TPU v7x, 32 devices: a whole 2x2x4 slice. The times are simulated.
32 devices in a mesh: grp: 8 (over z, x), crm: 4 (over y, core).
Axes of the slice: x: 2, y: 2, z: 4, core: 2. Of those that a mesh axis runs over, the one named last changes fastest.
Arguments:
- crm_state: float32 [1152, 3, 3712], P(('grp', 'crm')), may hold values from -6 to 6
- forcing: float32 [768, 2, 72], P(('grp', 'crm')), may hold values from -6 to 6
- target: int32 [768], P(('grp', 'crm')), may hold values from 0 to 3, as said below
- cost_class: int32 [768], P(('grp', 'crm')), may hold values from 1 to 3
- level_map: float32 [58, 72], replicated, may hold values from 0 to 0.4, as said below
- remap_index: int32 [768, 4], P(('grp', 'crm')), may hold values from 0 to 71, as said below
- remap_weight: float32 [768, 4], P(('grp', 'crm')), may hold values from 0.2 to 1
Outputs:
- new_state: float32 [1152, 3, 3712], P(('grp', 'crm'))
- cloud_water: float32 [768, 3712], P(('grp', 'crm'))
- physics_tendency: float32 [768, 2, 72], P(('grp', 'crm'))
Inputs may be any that keep to these rules, and one draw needn't show every extreme that they name: `target`: of one owner device's columns at most 9 name the same worker; in every group one worker receives exactly 9 columns from each of the group's 4 owners. `remap_index`: entry 0 names a column of the block before the cell's own, entry 1 one of its own block (offset 24), entry 2 one of the block after (offset 2 * 24), entry 3 any of the three. `level_map`: zero except within two GCM levels of the level nearest to each model level.
All inputs are finite; a program needn't handle non-finite values.
Results may differ from a plain program's by a relative error of at most 0.0003.
Values sent between devices are 32-bit elements; how exact they have to be, the bound alone decides.
No kernel may reach another device: no remote copies, remote signals or barrier semaphores. Data moves between devices by JAX's collectives and lax.ppermute only.
A program may use at most 64 MiB of HBM per device.

v0:
```python
import jax
import jax.numpy as jnp
from jax import lax
from jax.sharding import PartitionSpec as P

CLASSES = 3
SUB = 4


DIFFUSE_HORIZ = 0.2
DIFFUSE_VERT = 0.1
CONDENSE_RATE = 3.0
LINEAR_DRAG = 0.1
MOIST_BUOYANCY = 0.6
HIGHEST = lax.Precision.HIGHEST


def extended_2(x, sides, width):
    for axis, dim in sides:
        size, length = (lax.axis_size(axis), x.shape[dim])
        up = [(i, (i + 1) % size) for i in range(size)]
        down = [(j, i) for i, j in up]
        last = lax.slice_in_dim(x, length - width, length, axis=dim)
        first = lax.slice_in_dim(x, 0, width, axis=dim)
        before = lax.ppermute(last, axis, up)
        after = lax.ppermute(first, axis, down)
        x = jnp.concatenate([before, x, after], axis=dim)
    return x


def cell_tables(levels_crm, columns_crm):
    cell_count = levels_crm * columns_crm
    cell_ids = jnp.arange(cell_count)
    level_of = cell_ids // columns_crm
    column_of = cell_ids % columns_crm
    level_ids = jnp.arange(levels_crm)
    average = (level_of[:, None] == level_ids[None, :]).astype(jnp.float32) / columns_crm
    spreader = (level_ids[:, None] == level_of[None, :]).astype(jnp.float32)
    saturated = 1.0 - 2.0 * (level_of.astype(jnp.float32) + 0.5) / levels_crm
    return {
        "average": average,
        "spreader": spreader,
        "saturated": saturated,
        "top": level_of == levels_crm - 1,
        "bottom": level_of == 0,
        "first": column_of == 0,
        "last": column_of == columns_crm - 1,
        "width": columns_crm,
    }


def level_mean(field, tables):
    means = jnp.dot(field, tables["average"], precision=HIGHEST)
    return jnp.dot(means, tables["spreader"], precision=HIGHEST)


def vertical_terms(field, tables):
    width = tables["width"]
    above = jnp.where(tables["top"][None, :], 0.0, jnp.roll(field, -width, -1))
    below = jnp.where(tables["bottom"][None, :], 0.0, jnp.roll(field, width, -1))
    return (0.5 * (above - below), above + below - 2.0 * field)


def horizontal_lap(field, tables):
    width = tables["width"]
    left = jnp.where(
        tables["first"][None, :], jnp.roll(field, -(width - 1), -1), jnp.roll(field, 1, -1)
    )
    right = jnp.where(
        tables["last"][None, :], jnp.roll(field, width - 1, -1), jnp.roll(field, -1, -1)
    )
    return left + right - 2.0 * field


def substep(fields, force_theta, force_moist, step_grid, tables):
    theta_field, moist, vertical = fields
    buoyancy = theta_field + MOIST_BUOYANCY * moist
    condensed = CONDENSE_RATE * jnp.maximum(moist - tables["saturated"][None, :], 0.0)
    theta_grad, theta_lapz = vertical_terms(theta_field, tables)
    moist_grad, moist_lapz = vertical_terms(moist, tables)
    vert_grad, vert_lapz = vertical_terms(vertical, tables)
    new_theta = theta_field + step_grid * (
        -vertical * theta_grad
        + DIFFUSE_HORIZ * horizontal_lap(theta_field, tables)
        + DIFFUSE_VERT * theta_lapz
        + force_theta
        + condensed
    )
    new_moist = moist + step_grid * (
        -vertical * moist_grad
        + DIFFUSE_HORIZ * horizontal_lap(moist, tables)
        + DIFFUSE_VERT * moist_lapz
        + force_moist
        - condensed
    )
    pushed = vertical + step_grid * (
        buoyancy
        - level_mean(buoyancy, tables)
        + DIFFUSE_HORIZ * horizontal_lap(vertical, tables)
        + DIFFUSE_VERT * vert_lapz
        - LINEAR_DRAG * vertical
    )
    new_vertical = pushed - level_mean(pushed, tables)
    return (new_theta, new_moist, new_vertical)


def run_models(crm_state, crm_forcing, class_value, total_steps, tables):
    steps_here = class_value * SUB
    step_grid = (1.0 / jnp.maximum(steps_here, 1.0))[:, None]
    force_theta = jnp.dot(crm_forcing[:, 0], tables["spreader"], precision=HIGHEST)
    force_moist = jnp.dot(crm_forcing[:, 1], tables["spreader"], precision=HIGHEST)
    begin = (crm_state[:, 0], crm_state[:, 1], crm_state[:, 2])

    def advance(index_step, fields):
        moved = substep(fields, force_theta, force_moist, step_grid, tables)
        live = (index_step.astype(jnp.float32) < steps_here)[:, None]
        return tuple(
            (jnp.where(live, new_field, old_field) for new_field, old_field in zip(moved, fields))
        )

    return (begin, lax.fori_loop(0, total_steps, advance, begin))


def body(crm_state, forcing, target, cost_class, level_map, remap_index, remap_weight):
    workers = lax.axis_size("crm")
    col_dev = forcing.shape[0]
    slots_dev = crm_state.shape[0]
    capacity = slots_dev // workers
    levels_crm, levels_gcm = level_map.shape
    cell_count = crm_state.shape[2]
    columns_crm = cell_count // levels_crm
    tables = cell_tables(levels_crm, columns_crm)
    onehot = (target[:, None] == jnp.arange(workers)[None, :]).astype(jnp.int32)
    before = jnp.cumsum(onehot, axis=0) - onehot
    slot_rank = jnp.sum(before * onehot, axis=1)
    slot_flat = target * capacity + slot_rank
    mapped = jnp.einsum("kj,cvj->cvk", level_map, forcing, precision=HIGHEST)
    outgoing = mapped.reshape(col_dev, 2 * levels_crm)
    send_width = outgoing.shape[1]
    send_forcing = jnp.zeros((slots_dev, send_width), jnp.float32).at[slot_flat].set(outgoing)
    send_class = (
        jnp.zeros((slots_dev,), jnp.float32).at[slot_flat].set(cost_class.astype(jnp.float32))
    )
    got_forcing, got_class = (
        lax.all_to_all(
            send_forcing.reshape(workers, capacity, send_width),
            "crm",
            split_axis=0,
            concat_axis=0,
            tiled=True,
        ),
        lax.all_to_all(
            send_class.reshape(workers, capacity), "crm", split_axis=0, concat_axis=0, tiled=True
        ),
    )
    got_forcing = got_forcing.reshape(slots_dev, 2, -1)
    got_class = got_class.reshape(slots_dev)
    begin, ended = run_models(crm_state, got_forcing, got_class, CLASSES * SUB, tables)
    theta_change = jnp.dot(ended[0] - begin[0], tables["average"], precision=HIGHEST)
    moist_change = jnp.dot(ended[1] - begin[1], tables["average"], precision=HIGHEST)
    tendency = jnp.stack([theta_change, moist_change], axis=1)
    condensate = jnp.maximum(ended[1] - tables["saturated"][None, :], 0.0)
    back_tendency = tendency.reshape(slots_dev, -1)
    returned_tendency, returned_cloud = (
        lax.all_to_all(
            back_tendency.reshape(workers, capacity, -1),
            "crm",
            split_axis=0,
            concat_axis=0,
            tiled=True,
        ),
        lax.all_to_all(
            condensate.reshape(workers, capacity, cell_count),
            "crm",
            split_axis=0,
            concat_axis=0,
            tiled=True,
        ),
    )
    owned_tendency = returned_tendency.reshape(slots_dev, -1)[slot_flat]
    gcm_tendency = jnp.einsum(
        "kj,cvk->cvj", level_map, owned_tendency.reshape(col_dev, 2, levels_crm), precision=HIGHEST
    )
    source_ids = jnp.arange(3 * col_dev)
    remap_matrix = jnp.sum(
        remap_weight[:, :, None]
        * (remap_index[:, :, None] == source_ids[None, None, :]).astype(jnp.float32),
        axis=1,
    )
    weight_total = jnp.sum(remap_weight, axis=1)
    extended = extended_2(gcm_tendency, ((("grp", "crm"), 0),), col_dev)
    weighted = jnp.einsum("cr,rvj->cvj", remap_matrix, extended, precision=HIGHEST)
    physics_tendency = weighted / weight_total[:, None, None]
    cloud_water = returned_cloud.reshape(slots_dev, cell_count)[slot_flat]
    new_state = jnp.stack([ended[0], ended[1], ended[2]], axis=1)
    return (new_state, cloud_water, physics_tendency)


def solution(mesh):
    in_specs = (
        P(("grp", "crm"), None, None),
        P(("grp", "crm"), None, None),
        P(("grp", "crm")),
        P(("grp", "crm")),
        P(),
        P(("grp", "crm"), None),
        P(("grp", "crm"), None),
    )
    out_specs = (
        P(("grp", "crm"), None, None),
        P(("grp", "crm"), None),
        P(("grp", "crm"), None, None),
    )
    return jax.shard_map(body, mesh=mesh, in_specs=in_specs, out_specs=out_specs, check_vma=False)
```

profile of v0, /device:TPU:0, one launch (start us, length us, event | category | flops | bytes accessed | tf_op | source)
XLA Modules:
  0.0 270.3 jit_solution(2440567595162227622)
XLA Ops:
  4.9 4.2 %all-to-all-start = ((f32[4,1,9]{2,1,0:T(1,128)}), f32[4,1,9]{2,1,0:T(1,128)S(1)}, u32[]{:S(2)}, u32[]{:S(2)}) async-start(f32[4,1,9]{2,1,0:T(1,128)} %bitcast.3), calls=%async_computation | async-start | bytes 4096 | tf_op jit(solution)/shard_map/all_to_all | solution.py:152
  10.2 1.6 slice_bitcast_fusion
  13.2 3.3 %all-to-all-start.1 = ((f32[4,9,116]{2,1,0:T(8,128)}), f32[4,9,116]{2,1,0:T(8,128)S(1)}, u32[]{:S(2)}, u32[]{:S(2)}) async-start(f32[4,9,116]{2,1,0:T(8,128)} %reshape.105), calls=%async_computation.1 | async-start | bytes 65536 | tf_op jit(solution)/shard_map/all_to_all | solution.py:145
  16.7 3.7 %all-to-all-done.1 = f32[4,9,116]{2,1,0:T(8,128)S(1)} async-done(((f32[4,9,116]{2,1,0:T(8,128)}), f32[4,9,116]{2,1,0:T(8,128)S(1)}, u32[]{:S(2)}, u32[]{:S(2)}) %all-to-all-start.1) | async-done | bytes 16736 | tf_op jit(solution)/shard_map/all_to_all | solution.py:145
  23.1 215.5 %while.20 = (s32[]{:T(128)}, f32[36,3712]{1,0:T(8,128)S(1)}, f32[36,3712]{1,0:T(8,128)S(1)}, f32[36,3712]{1,0:T(8,128)S(1)}, f32[36]{0:T(128)S(1)}, /*index=5*/f...) while((s32[]{:T(128)}, f32[36,3712]{1,0:T(8,128)S(1)}, ...), condition=%wide.region_5.6_spmd.clone.clone.clone, body=%wide.region_4.5_spmd.clone.clone.clone.sunk | while | flops 386159392 | bytes 51972072 | solution.py:121
  23.5 1.5 fusion.193
  28.2 2.4 fusion.198
  34.5 3.1 %add_select_fusion.6 = f32[36,3712]{1,0:T(8,128)S(1)} fusion(f32[36,3712]{1,0:T(8,128)S(1)} %get-tuple-element.628, f32[36,3712]{1,0:T(8,128)} %get-tuple-element.643, f32[36,63]{1,0:T(8,128)S(1)} %get-tuple-element.577, f32[36,3649]{1,0:T(8,128)} %get-tuple-element.578, f32[36,3711]{1,0:T(8,128)} %get-tuple-element.579, ...), kind=kLoop, calls=%fused_computation.34.clone.1 | loop fusion | flops 4142592 | bytes 5909684 | tf_op jit(solution)/shard_map/while/body/eval_jaxpr/jit(_where)/select_n | solution.py:118
  41.5 1.5 fusion.193
  46.2 2.4 fusion.198
  52.4 3.1 %add_select_fusion.6 = f32[36,3712]{1,0:T(8,128)S(1)} fusion(f32[36,3712]{1,0:T(8,128)S(1)} %get-tuple-element.628, f32[36,3712]{1,0:T(8,128)} %get-tuple-element.643, f32[36,63]{1,0:T(8,128)S(1)} %get-tuple-element.577, f32[36,3649]{1,0:T(8,128)} %get-tuple-element.578, f32[36,3711]{1,0:T(8,128)} %get-tuple-element.579, ...), kind=kLoop, calls=%fused_computation.34.clone.1 | loop fusion | flops 4142592 | bytes 5909684 | tf_op jit(solution)/shard_map/while/body/eval_jaxpr/jit(_where)/select_n | solution.py:118
  59.4 1.5 fusion.193
  64.1 2.4 fusion.198
  70.3 3.1 %add_select_fusion.6 = f32[36,3712]{1,0:T(8,128)S(1)} fusion(f32[36,3712]{1,0:T(8,128)S(1)} %get-tuple-element.628, f32[36,3712]{1,0:T(8,128)} %get-tuple-element.643, f32[36,63]{1,0:T(8,128)S(1)} %get-tuple-element.577, f32[36,3649]{1,0:T(8,128)} %get-tuple-element.578, f32[36,3711]{1,0:T(8,128)} %get-tuple-element.579, ...), kind=kLoop, calls=%fused_computation.34.clone.1 | loop fusion | flops 4142592 | bytes 5909684 | tf_op jit(solution)/shard_map/while/body/eval_jaxpr/jit(_where)/select_n | solution.py:118
  77.4 1.5 fusion.193
  82.0 2.4 fusion.198
  88.3 3.1 %add_select_fusion.6 = f32[36,3712]{1,0:T(8,128)S(1)} fusion(f32[36,3712]{1,0:T(8,128)S(1)} %get-tuple-element.628, f32[36,3712]{1,0:T(8,128)} %get-tuple-element.643, f32[36,63]{1,0:T(8,128)S(1)} %get-tuple-element.577, f32[36,3649]{1,0:T(8,128)} %get-tuple-element.578, f32[36,3711]{1,0:T(8,128)} %get-tuple-element.579, ...), kind=kLoop, calls=%fused_computation.34.clone.1 | loop fusion | flops 4142592 | bytes 5909684 | tf_op jit(solution)/shard_map/while/body/eval_jaxpr/jit(_where)/select_n | solution.py:118
  95.3 1.5 fusion.193
  100.0 2.4 fusion.198
  106.2 3.1 %add_select_fusion.6 = f32[36,3712]{1,0:T(8,128)S(1)} fusion(f32[36,3712]{1,0:T(8,128)S(1)} %get-tuple-element.628, f32[36,3712]{1,0:T(8,128)} %get-tuple-element.643, f32[36,63]{1,0:T(8,128)S(1)} %get-tuple-element.577, f32[36,3649]{1,0:T(8,128)} %get-tuple-element.578, f32[36,3711]{1,0:T(8,128)} %get-tuple-element.579, ...), kind=kLoop, calls=%fused_computation.34.clone.1 | loop fusion | flops 4142592 | bytes 5909684 | tf_op jit(solution)/shard_map/while/body/eval_jaxpr/jit(_where)/select_n | solution.py:118
  113.3 1.5 fusion.193
  117.9 2.4 fusion.198
  124.2 3.1 %add_select_fusion.6 = f32[36,3712]{1,0:T(8,128)S(1)} fusion(f32[36,3712]{1,0:T(8,128)S(1)} %get-tuple-element.628, f32[36,3712]{1,0:T(8,128)} %get-tuple-element.643, f32[36,63]{1,0:T(8,128)S(1)} %get-tuple-element.577, f32[36,3649]{1,0:T(8,128)} %get-tuple-element.578, f32[36,3711]{1,0:T(8,128)} %get-tuple-element.579, ...), kind=kLoop, calls=%fused_computation.34.clone.1 | loop fusion | flops 4142592 | bytes 5909684 | tf_op jit(solution)/shard_map/while/body/eval_jaxpr/jit(_where)/select_n | solution.py:118
  131.2 1.5 fusion.193
  135.9 2.4 fusion.198
  142.1 3.1 %add_select_fusion.6 = f32[36,3712]{1,0:T(8,128)S(1)} fusion(f32[36,3712]{1,0:T(8,128)S(1)} %get-tuple-element.628, f32[36,3712]{1,0:T(8,128)} %get-tuple-element.643, f32[36,63]{1,0:T(8,128)S(1)} %get-tuple-element.577, f32[36,3649]{1,0:T(8,128)} %get-tuple-element.578, f32[36,3711]{1,0:T(8,128)} %get-tuple-element.579, ...), kind=kLoop, calls=%fused_computation.34.clone.1 | loop fusion | flops 4142592 | bytes 5909684 | tf_op jit(solution)/shard_map/while/body/eval_jaxpr/jit(_where)/select_n | solution.py:118
  149.2 1.5 fusion.193
  153.8 2.4 fusion.198
  160.1 3.1 %add_select_fusion.6 = f32[36,3712]{1,0:T(8,128)S(1)} fusion(f32[36,3712]{1,0:T(8,128)S(1)} %get-tuple-element.628, f32[36,3712]{1,0:T(8,128)} %get-tuple-element.643, f32[36,63]{1,0:T(8,128)S(1)} %get-tuple-element.577, f32[36,3649]{1,0:T(8,128)} %get-tuple-element.578, f32[36,3711]{1,0:T(8,128)} %get-tuple-element.579, ...), kind=kLoop, calls=%fused_computation.34.clone.1 | loop fusion | flops 4142592 | bytes 5909684 | tf_op jit(solution)/shard_map/while/body/eval_jaxpr/jit(_where)/select_n | solution.py:118
  167.1 1.5 fusion.193
  171.8 2.4 fusion.198
  178.0 3.1 %add_select_fusion.6 = f32[36,3712]{1,0:T(8,128)S(1)} fusion(f32[36,3712]{1,0:T(8,128)S(1)} %get-tuple-element.628, f32[36,3712]{1,0:T(8,128)} %get-tuple-element.643, f32[36,63]{1,0:T(8,128)S(1)} %get-tuple-element.577, f32[36,3649]{1,0:T(8,128)} %get-tuple-element.578, f32[36,3711]{1,0:T(8,128)} %get-tuple-element.579, ...), kind=kLoop, calls=%fused_computation.34.clone.1 | loop fusion | flops 4142592 | bytes 5909684 | tf_op jit(solution)/shard_map/while/body/eval_jaxpr/jit(_where)/select_n | solution.py:118
  185.1 1.5 fusion.193
  189.7 2.4 fusion.198
  196.0 3.1 %add_select_fusion.6 = f32[36,3712]{1,0:T(8,128)S(1)} fusion(f32[36,3712]{1,0:T(8,128)S(1)} %get-tuple-element.628, f32[36,3712]{1,0:T(8,128)} %get-tuple-element.643, f32[36,63]{1,0:T(8,128)S(1)} %get-tuple-element.577, f32[36,3649]{1,0:T(8,128)} %get-tuple-element.578, f32[36,3711]{1,0:T(8,128)} %get-tuple-element.579, ...), kind=kLoop, calls=%fused_computation.34.clone.1 | loop fusion | flops 4142592 | bytes 5909684 | tf_op jit(solution)/shard_map/while/body/eval_jaxpr/jit(_where)/select_n | solution.py:118
  203.0 1.5 fusion.193
  207.7 2.4 fusion.198
  213.9 3.1 %add_select_fusion.6 = f32[36,3712]{1,0:T(8,128)S(1)} fusion(f32[36,3712]{1,0:T(8,128)S(1)} %get-tuple-element.628, f32[36,3712]{1,0:T(8,128)} %get-tuple-element.643, f32[36,63]{1,0:T(8,128)S(1)} %get-tuple-element.577, f32[36,3649]{1,0:T(8,128)} %get-tuple-element.578, f32[36,3711]{1,0:T(8,128)} %get-tuple-element.579, ...), kind=kLoop, calls=%fused_computation.34.clone.1 | loop fusion | flops 4142592 | bytes 5909684 | tf_op jit(solution)/shard_map/while/body/eval_jaxpr/jit(_where)/select_n | solution.py:118
  220.9 1.5 fusion.193
  225.6 2.4 fusion.198
  231.9 3.1 %add_select_fusion.6 = f32[36,3712]{1,0:T(8,128)S(1)} fusion(f32[36,3712]{1,0:T(8,128)S(1)} %get-tuple-element.628, f32[36,3712]{1,0:T(8,128)} %get-tuple-element.643, f32[36,63]{1,0:T(8,128)S(1)} %get-tuple-element.577, f32[36,3649]{1,0:T(8,128)} %get-tuple-element.578, f32[36,3711]{1,0:T(8,128)} %get-tuple-element.579, ...), kind=kLoop, calls=%fused_computation.34.clone.1 | loop fusion | flops 4142592 | bytes 5909684 | tf_op jit(solution)/shard_map/while/body/eval_jaxpr/jit(_where)/select_n | solution.py:118
  238.6 2.5 fusion.80
  241.2 2.5 fusion.83
  244.5 3.3 %all-to-all-start.3 = ((f32[4,9,116]{2,1,0:T(8,128)}), f32[4,9,116]{2,1,0:T(8,128)S(1)}, u32[]{:S(2)}, u32[]{:S(2)}) async-start(f32[4,9,116]{2,1,0:T(8,128)} %reshape_reshape.3), calls=%async_computation.3 | async-start | bytes 65536 | tf_op jit(solution)/shard_map/all_to_all | solution.py:165
  248.8 2.8 %all-to-all-done.3 = f32[4,9,116]{2,1,0:T(8,128)S(1)} async-done(((f32[4,9,116]{2,1,0:T(8,128)}), f32[4,9,116]{2,1,0:T(8,128)S(1)}, u32[]{:S(2)}, u32[]{:S(2)}) %all-to-all-start.3) | async-done | bytes 16736 | tf_op jit(solution)/shard_map/all_to_all | solution.py:165
  251.6 3.5 %all-to-all-start.2 = ((f32[4,9,3712]{2,1,0:T(8,128)}), f32[4,9,3712]{2,1,0:T(8,128)S(1)}, u32[]{:S(2)}, u32[]{:S(2)}) async-start(f32[4,9,3712]{2,1,0:T(8,128)} %reshape.107), calls=%async_computation.2 | async-start | bytes 1900544 | tf_op jit(solution)/shard_map/all_to_all | solution.py:172
  256.5 5.7 %collective-permute-start.1 = (f32[24,2,72]{2,0,1:T(8,128)S(1)}, f32[24,2,72]{2,0,1:T(8,128)S(1)}, u32[]{:S(2)}, u32[]{:S(2)}) collective-permute-start(f32[24,2,72]{2,0,1:T(8,128)S(1)} %fusion.103), channel_id=1, source_target_pairs={{1,0},{2,1},{3,2},{4,3},{5,4},{6,5},{7,6},{8,7},{9,8},{10,9},{11,1... | collective-permute-start | bytes 41480 | tf_op jit(solution)/shard_map/ppermute | solution.py:26
  264.6 4.2 %all-to-all-done.2 = f32[4,9,3712]{2,1,0:T(8,128)S(1)} async-done(((f32[4,9,3712]{2,1,0:T(8,128)}), f32[4,9,3712]{2,1,0:T(8,128)S(1)}, u32[]{:S(2)}, u32[]{:S(2)}) %all-to-all-start.2) | async-done | bytes 534560 | tf_op jit(solution)/shard_map/all_to_all | solution.py:172
  (420 shorter events, 146.6 us)
Async XLA Ops:
  0.6 8.5 %copy-start = (f32[58,72]{1,0:T(8,128)S(1)}, f32[58,72]{1,0:T(8,128)}, u32[]{:S(2)}) copy-start(f32[58,72]{1,0:T(8,128)} %param.13) | copy-start | bytes 50116
  4.9 8.3 %all-to-all-start = ((f32[4,1,9]{2,1,0:T(1,128)}), f32[4,1,9]{2,1,0:T(1,128)S(1)}, u32[]{:S(2)}, u32[]{:S(2)}) async-start(f32[4,1,9]{2,1,0:T(1,128)} %bitcast.3), calls=%async_computation | async-start | bytes 4096 | tf_op jit(solution)/shard_map/all_to_all | solution.py:152
  13.2 7.2 %all-to-all-start.1 = ((f32[4,9,116]{2,1,0:T(8,128)}), f32[4,9,116]{2,1,0:T(8,128)S(1)}, u32[]{:S(2)}, u32[]{:S(2)}) async-start(f32[4,9,116]{2,1,0:T(8,128)} %reshape.105), calls=%async_computation.1 | async-start | bytes 65536 | tf_op jit(solution)/shard_map/all_to_all | solution.py:145
  34.4 3.2 %copy-start.1 = (f32[36,3711]{1,0:T(8,128)S(1)}, f32[36,3711]{1,0:T(8,128)}, u32[]{:S(2)}) copy-start(f32[36,3711]{1,0:T(8,128)} %get-tuple-element.595) | copy-start | bytes 1603156 | tf_op jit(solution)/shard_map/while
  34.4 3.2 %copy-start.2 = (f32[36,3711]{1,0:T(8,128)S(1)}, f32[36,3711]{1,0:T(8,128)}, u32[]{:S(2)}) copy-start(f32[36,3711]{1,0:T(8,128)} %get-tuple-element.600) | copy-start | bytes 1603156 | tf_op jit(solution)/shard_map/while
  34.4 3.2 %copy-start.3 = (f32[36,3648]{1,0:T(8,128)S(1)}, f32[36,3648]{1,0:T(8,128)}, u32[]{:S(2)}) copy-start(f32[36,3648]{1,0:T(8,128)} %get-tuple-element.601) | copy-start | bytes 1575940 | tf_op jit(solution)/shard_map/while
  34.4 3.2 %copy-start.4 = (f32[36,3648]{1,0:T(8,128)S(1)}, f32[36,3648]{1,0:T(8,128)}, u32[]{:S(2)}) copy-start(f32[36,3648]{1,0:T(8,128)} %get-tuple-element.604) | copy-start | bytes 1575940 | tf_op jit(solution)/shard_map/while
  34.4 3.2 %copy-start.5 = (f32[36,3712]{1,0:T(8,128)S(1)}, f32[36,3712]{1,0:T(8,128)}, u32[]{:S(2)}) copy-start(f32[36,3712]{1,0:T(8,128)} %get-tuple-element.644) | copy-start | bytes 1603588 | tf_op jit(solution)/shard_map/while
  52.4 3.2 %copy-start.1 = (f32[36,3711]{1,0:T(8,128)S(1)}, f32[36,3711]{1,0:T(8,128)}, u32[]{:S(2)}) copy-start(f32[36,3711]{1,0:T(8,128)} %get-tuple-element.595) | copy-start | bytes 1603156 | tf_op jit(solution)/shard_map/while
  52.4 3.2 %copy-start.2 = (f32[36,3711]{1,0:T(8,128)S(1)}, f32[36,3711]{1,0:T(8,128)}, u32[]{:S(2)}) copy-start(f32[36,3711]{1,0:T(8,128)} %get-tuple-element.600) | copy-start | bytes 1603156 | tf_op jit(solution)/shard_map/while
  52.4 3.2 %copy-start.3 = (f32[36,3648]{1,0:T(8,128)S(1)}, f32[36,3648]{1,0:T(8,128)}, u32[]{:S(2)}) copy-start(f32[36,3648]{1,0:T(8,128)} %get-tuple-element.601) | copy-start | bytes 1575940 | tf_op jit(solution)/shard_map/while
  52.4 3.2 %copy-start.4 = (f32[36,3648]{1,0:T(8,128)S(1)}, f32[36,3648]{1,0:T(8,128)}, u32[]{:S(2)}) copy-start(f32[36,3648]{1,0:T(8,128)} %get-tuple-element.604) | copy-start | bytes 1575940 | tf_op jit(solution)/shard_map/while
  52.4 3.2 %copy-start.5 = (f32[36,3712]{1,0:T(8,128)S(1)}, f32[36,3712]{1,0:T(8,128)}, u32[]{:S(2)}) copy-start(f32[36,3712]{1,0:T(8,128)} %get-tuple-element.644) | copy-start | bytes 1603588 | tf_op jit(solution)/shard_map/while
  70.3 3.2 %copy-start.1 = (f32[36,3711]{1,0:T(8,128)S(1)}, f32[36,3711]{1,0:T(8,128)}, u32[]{:S(2)}) copy-start(f32[36,3711]{1,0:T(8,128)} %get-tuple-element.595) | copy-start | bytes 1603156 | tf_op jit(solution)/shard_map/while
  70.3 3.2 %copy-start.2 = (f32[36,3711]{1,0:T(8,128)S(1)}, f32[36,3711]{1,0:T(8,128)}, u32[]{:S(2)}) copy-start(f32[36,3711]{1,0:T(8,128)} %get-tuple-element.600) | copy-start | bytes 1603156 | tf_op jit(solution)/shard_map/while
  70.3 3.2 %copy-start.3 = (f32[36,3648]{1,0:T(8,128)S(1)}, f32[36,3648]{1,0:T(8,128)}, u32[]{:S(2)}) copy-start(f32[36,3648]{1,0:T(8,128)} %get-tuple-element.601) | copy-start | bytes 1575940 | tf_op jit(solution)/shard_map/while
  70.3 3.2 %copy-start.4 = (f32[36,3648]{1,0:T(8,128)S(1)}, f32[36,3648]{1,0:T(8,128)}, u32[]{:S(2)}) copy-start(f32[36,3648]{1,0:T(8,128)} %get-tuple-element.604) | copy-start | bytes 1575940 | tf_op jit(solution)/shard_map/while
  70.3 3.2 %copy-start.5 = (f32[36,3712]{1,0:T(8,128)S(1)}, f32[36,3712]{1,0:T(8,128)}, u32[]{:S(2)}) copy-start(f32[36,3712]{1,0:T(8,128)} %get-tuple-element.644) | copy-start | bytes 1603588 | tf_op jit(solution)/shard_map/while
  88.2 3.2 %copy-start.1 = (f32[36,3711]{1,0:T(8,128)S(1)}, f32[36,3711]{1,0:T(8,128)}, u32[]{:S(2)}) copy-start(f32[36,3711]{1,0:T(8,128)} %get-tuple-element.595) | copy-start | bytes 1603156 | tf_op jit(solution)/shard_map/while
  88.3 3.2 %copy-start.2 = (f32[36,3711]{1,0:T(8,128)S(1)}, f32[36,3711]{1,0:T(8,128)}, u32[]{:S(2)}) copy-start(f32[36,3711]{1,0:T(8,128)} %get-tuple-element.600) | copy-start | bytes 1603156 | tf_op jit(solution)/shard_map/while
  88.3 3.2 %copy-start.3 = (f32[36,3648]{1,0:T(8,128)S(1)}, f32[36,3648]{1,0:T(8,128)}, u32[]{:S(2)}) copy-start(f32[36,3648]{1,0:T(8,128)} %get-tuple-element.601) | copy-start | bytes 1575940 | tf_op jit(solution)/shard_map/while
  88.3 3.2 %copy-start.4 = (f32[36,3648]{1,0:T(8,128)S(1)}, f32[36,3648]{1,0:T(8,128)}, u32[]{:S(2)}) copy-start(f32[36,3648]{1,0:T(8,128)} %get-tuple-element.604) | copy-start | bytes 1575940 | tf_op jit(solution)/shard_map/while
  88.3 3.2 %copy-start.5 = (f32[36,3712]{1,0:T(8,128)S(1)}, f32[36,3712]{1,0:T(8,128)}, u32[]{:S(2)}) copy-start(f32[36,3712]{1,0:T(8,128)} %get-tuple-element.644) | copy-start | bytes 1603588 | tf_op jit(solution)/shard_map/while
  106.2 3.2 %copy-start.1 = (f32[36,3711]{1,0:T(8,128)S(1)}, f32[36,3711]{1,0:T(8,128)}, u32[]{:S(2)}) copy-start(f32[36,3711]{1,0:T(8,128)} %get-tuple-element.595) | copy-start | bytes 1603156 | tf_op jit(solution)/shard_map/while
  106.2 3.2 %copy-start.2 = (f32[36,3711]{1,0:T(8,128)S(1)}, f32[36,3711]{1,0:T(8,128)}, u32[]{:S(2)}) copy-start(f32[36,3711]{1,0:T(8,128)} %get-tuple-element.600) | copy-start | bytes 1603156 | tf_op jit(solution)/shard_map/while
  106.2 3.2 %copy-start.3 = (f32[36,3648]{1,0:T(8,128)S(1)}, f32[36,3648]{1,0:T(8,128)}, u32[]{:S(2)}) copy-start(f32[36,3648]{1,0:T(8,128)} %get-tuple-element.601) | copy-start | bytes 1575940 | tf_op jit(solution)/shard_map/while
  106.2 3.2 %copy-start.4 = (f32[36,3648]{1,0:T(8,128)S(1)}, f32[36,3648]{1,0:T(8,128)}, u32[]{:S(2)}) copy-start(f32[36,3648]{1,0:T(8,128)} %get-tuple-element.604) | copy-start | bytes 1575940 | tf_op jit(solution)/shard_map/while
  106.2 3.2 %copy-start.5 = (f32[36,3712]{1,0:T(8,128)S(1)}, f32[36,3712]{1,0:T(8,128)}, u32[]{:S(2)}) copy-start(f32[36,3712]{1,0:T(8,128)} %get-tuple-element.644) | copy-start | bytes 1603588 | tf_op jit(solution)/shard_map/while
  124.1 3.2 %copy-start.1 = (f32[36,3711]{1,0:T(8,128)S(1)}, f32[36,3711]{1,0:T(8,128)}, u32[]{:S(2)}) copy-start(f32[36,3711]{1,0:T(8,128)} %get-tuple-element.595) | copy-start | bytes 1603156 | tf_op jit(solution)/shard_map/while
  160.0 3.2 %copy-start.1 = (f32[36,3711]{1,0:T(8,128)S(1)}, f32[36,3711]{1,0:T(8,128)}, u32[]{:S(2)}) copy-start(f32[36,3711]{1,0:T(8,128)} %get-tuple-element.595) | copy-start | bytes 1603156 | tf_op jit(solution)/shard_map/while
  160.0 3.2 %copy-start.2 = (f32[36,3711]{1,0:T(8,128)S(1)}, f32[36,3711]{1,0:T(8,128)}, u32[]{:S(2)}) copy-start(f32[36,3711]{1,0:T(8,128)} %get-tuple-element.600) | copy-start | bytes 1603156 | tf_op jit(solution)/shard_map/while
  160.0 3.2 %copy-start.3 = (f32[36,3648]{1,0:T(8,128)S(1)}, f32[36,3648]{1,0:T(8,128)}, u32[]{:S(2)}) copy-start(f32[36,3648]{1,0:T(8,128)} %get-tuple-element.601) | copy-start | bytes 1575940 | tf_op jit(solution)/shard_map/while
  160.1 3.2 %copy-start.4 = (f32[36,3648]{1,0:T(8,128)S(1)}, f32[36,3648]{1,0:T(8,128)}, u32[]{:S(2)}) copy-start(f32[36,3648]{1,0:T(8,128)} %get-tuple-element.604) | copy-start | bytes 1575940 | tf_op jit(solution)/shard_map/while
  160.1 3.2 %copy-start.5 = (f32[36,3712]{1,0:T(8,128)S(1)}, f32[36,3712]{1,0:T(8,128)}, u32[]{:S(2)}) copy-start(f32[36,3712]{1,0:T(8,128)} %get-tuple-element.644) | copy-start | bytes 1603588 | tf_op jit(solution)/shard_map/while
  178.0 3.2 %copy-start.1 = (f32[36,3711]{1,0:T(8,128)S(1)}, f32[36,3711]{1,0:T(8,128)}, u32[]{:S(2)}) copy-start(f32[36,3711]{1,0:T(8,128)} %get-tuple-element.595) | copy-start | bytes 1603156 | tf_op jit(solution)/shard_map/while
  178.0 3.2 %copy-start.2 = (f32[36,3711]{1,0:T(8,128)S(1)}, f32[36,3711]{1,0:T(8,128)}, u32[]{:S(2)}) copy-start(f32[36,3711]{1,0:T(8,128)} %get-tuple-element.600) | copy-start | bytes 1603156 | tf_op jit(solution)/shard_map/while
  178.0 3.2 %copy-start.3 = (f32[36,3648]{1,0:T(8,128)S(1)}, f32[36,3648]{1,0:T(8,128)}, u32[]{:S(2)}) copy-start(f32[36,3648]{1,0:T(8,128)} %get-tuple-element.601) | copy-start | bytes 1575940 | tf_op jit(solution)/shard_map/while
  178.0 3.2 %copy-start.4 = (f32[36,3648]{1,0:T(8,128)S(1)}, f32[36,3648]{1,0:T(8,128)}, u32[]{:S(2)}) copy-start(f32[36,3648]{1,0:T(8,128)} %get-tuple-element.604) | copy-start | bytes 1575940 | tf_op jit(solution)/shard_map/while
  178.0 3.2 %copy-start.5 = (f32[36,3712]{1,0:T(8,128)S(1)}, f32[36,3712]{1,0:T(8,128)}, u32[]{:S(2)}) copy-start(f32[36,3712]{1,0:T(8,128)} %get-tuple-element.644) | copy-start | bytes 1603588 | tf_op jit(solution)/shard_map/while
  195.9 3.2 %copy-start.1 = (f32[36,3711]{1,0:T(8,128)S(1)}, f32[36,3711]{1,0:T(8,128)}, u32[]{:S(2)}) copy-start(f32[36,3711]{1,0:T(8,128)} %get-tuple-element.595) | copy-start | bytes 1603156 | tf_op jit(solution)/shard_map/while
  195.9 3.2 %copy-start.2 = (f32[36,3711]{1,0:T(8,128)S(1)}, f32[36,3711]{1,0:T(8,128)}, u32[]{:S(2)}) copy-start(f32[36,3711]{1,0:T(8,128)} %get-tuple-element.600) | copy-start | bytes 1603156 | tf_op jit(solution)/shard_map/while
  195.9 3.2 %copy-start.3 = (f32[36,3648]{1,0:T(8,128)S(1)}, f32[36,3648]{1,0:T(8,128)}, u32[]{:S(2)}) copy-start(f32[36,3648]{1,0:T(8,128)} %get-tuple-element.601) | copy-start | bytes 1575940 | tf_op jit(solution)/shard_map/while
  195.9 3.2 %copy-start.4 = (f32[36,3648]{1,0:T(8,128)S(1)}, f32[36,3648]{1,0:T(8,128)}, u32[]{:S(2)}) copy-start(f32[36,3648]{1,0:T(8,128)} %get-tuple-element.604) | copy-start | bytes 1575940 | tf_op jit(solution)/shard_map/while
  196.0 3.2 %copy-start.5 = (f32[36,3712]{1,0:T(8,128)S(1)}, f32[36,3712]{1,0:T(8,128)}, u32[]{:S(2)}) copy-start(f32[36,3712]{1,0:T(8,128)} %get-tuple-element.644) | copy-start | bytes 1603588 | tf_op jit(solution)/shard_map/while
  244.5 7.2 %all-to-all-start.3 = ((f32[4,9,116]{2,1,0:T(8,128)}), f32[4,9,116]{2,1,0:T(8,128)S(1)}, u32[]{:S(2)}, u32[]{:S(2)}) async-start(f32[4,9,116]{2,1,0:T(8,128)} %reshape_reshape.3), calls=%async_computation.3 | async-start | bytes 65536 | tf_op jit(solution)/shard_map/all_to_all | solution.py:165
  251.6 17.2 %all-to-all-start.2 = ((f32[4,9,3712]{2,1,0:T(8,128)}), f32[4,9,3712]{2,1,0:T(8,128)S(1)}, u32[]{:S(2)}, u32[]{:S(2)}) async-start(f32[4,9,3712]{2,1,0:T(8,128)} %reshape.107), calls=%async_computation.2 | async-start | bytes 1900544 | tf_op jit(solution)/shard_map/all_to_all | solution.py:172
  256.0 7.8 %collective-permute-start = (f32[24,2,72]{2,0,1:T(8,128)S(1)}, f32[24,2,72]{2,0,1:T(8,128)S(1)}, u32[]{:S(2)}, u32[]{:S(2)}) collective-permute-start(f32[24,2,72]{2,0,1:T(8,128)S(1)} %fusion.103), channel_id=1, source_target_pairs={{0,1},{1,2},{2,3},{3,4},{4,5},{5,6},{6,7},{7,8},{8,9},{9,10},{10,1... | collective-permute-start | bytes 41480 | tf_op jit(solution)/shard_map/ppermute | solution.py:25
  256.5 7.3 %collective-permute-start.1 = (f32[24,2,72]{2,0,1:T(8,128)S(1)}, f32[24,2,72]{2,0,1:T(8,128)S(1)}, u32[]{:S(2)}, u32[]{:S(2)}) collective-permute-start(f32[24,2,72]{2,0,1:T(8,128)S(1)} %fusion.103), channel_id=1, source_target_pairs={{1,0},{2,1},{3,2},{4,3},{5,4},{6,5},{7,6},{8,7},{9,8},{10,9},{11,1... | collective-permute-start | bytes 41480 | tf_op jit(solution)/shard_map/ppermute | solution.py:26
  (33 other events, 76.1 us)
where the time goes:
time: 272 us; the launch traced here: 270 us
  local copies, waits for them, and re-layouts  100 us (37%)
  matrix products  83.1 us (31%)
  other arithmetic  52.3 us (19%)
  starting transfers between devices  20.5 us (8%)
  waiting for transfers between devices  11.1 us (4%)
    select_n x24, other arithmetic, advance(): jnp.where(live, new_field, old_field)  47.4 us
    dot_general x24, matrix products, level_mean(): return jnp.dot(means, tables['spreader'], precision=HIGHEST)  39.2 us
    dot_general x24, matrix products, level_mean(): means = jnp.dot(field, tables['average'], precision=HIGHEST)  35 us
    slice x48, local copies, waits for them, and re-layouts, horizontal_lap(): jnp.roll(field, -1, -1)  34 us
    slice x48, local copies, waits for them, and re-layouts, horizontal_lap(): jnp.roll(field, width - 1, -1)  21.1 us
    slice x24, local copies, waits for them, and re-layouts, vertical_terms(): jnp.roll(field, width, -1)  18.1 us
    slice x24, local copies, waits for them, and re-layouts, vertical_terms(): above = jnp.where(tables['top'][None, :], 0.0, jnp.roll(field, -width, -1))  15.3 us
    ppermute x1, starting transfers between devices, extended_2(): after = lax.ppermute(first, axis, down)  5.71 us
  transfers between devices with their start and end apart: 6, of which 4 were waited for; matrix products, arithmetic and copies ran while one was open for 3% of the time, Pallas kernels for 0%

commit v1 on v0

v1 whole, which is shorter than its diff:
```python
import functools

import jax
import jax.numpy as jnp
from jax import lax
from jax.experimental import pallas as pl
from jax.experimental.pallas import tpu as pltpu
from jax.sharding import PartitionSpec as P

CLASSES = 3
SUB = 4
DIFFUSE_HORIZ = 0.2
DIFFUSE_VERT = 0.1
CONDENSE_RATE = 3.0
LINEAR_DRAG = 0.1
MOIST_BUOYANCY = 0.6
HIGHEST = lax.Precision.HIGHEST
F32 = jnp.float32
LANES = 128
ROWS = 8
PHASES = 4
MIB = 1 << 20


def iota(shape, axis):
    return lax.broadcasted_iota(jnp.int32, shape, axis)


def dot_t(lhs, rhs):
    return lax.dot_general(lhs, rhs, (((0,), (0,)), ((), ())), precision=HIGHEST, preferred_element_type=F32)


def dot(lhs, rhs):
    return jnp.dot(lhs, rhs, precision=HIGHEST, preferred_element_type=F32)


def all_rows(x):
    x = x + pltpu.roll(x, 4, 0)
    x = x + pltpu.roll(x, 2, 0)
    return x + pltpu.roll(x, 1, 0)


def lanes_of(levels):
    base = 2 * levels
    return base, base + 1, base + 2, base + 3


def pack_kernel(capacity, workers, target, cost, forcing, level_map, rows, counts):
    levels, gcm = level_map.shape
    columns = forcing.shape[0]
    lane_class, lane_slot, lane_column, lane_owner = lanes_of(levels)
    me = lax.axis_index("crm")
    for worker in range(workers):
        counts[worker] = 0
    sub = iota((columns, LANES), 0)
    lane = iota((columns, LANES), 1)
    classes = jnp.zeros((columns, LANES), F32)
    slots = jnp.zeros((columns, LANES), F32)
    for column in range(columns):
        worker = target[column]
        rank = counts[worker]
        counts[worker] = rank + 1
        slot = (worker * workers + me) * capacity + rank
        classes = jnp.where(sub == column, cost[column].astype(F32), classes)
        slots = jnp.where(sub == column, slot.astype(F32), slots)
    spread_row = iota((levels, LANES), 0)
    spread_lane = iota((levels, LANES), 1)
    mapped = jnp.zeros((columns, LANES), F32)
    for variable in range(2):
        place = (spread_lane == spread_row + variable * levels).astype(F32)
        mapped = mapped + dot(forcing[:, variable, :], dot_t(level_map[...], place))
    meta = jnp.where(lane == lane_class, classes, 0.0)
    meta = jnp.where(lane == lane_slot, slots, meta)
    meta = jnp.where(lane == lane_column, (sub + 1).astype(F32), meta)
    meta = jnp.where(lane == lane_owner, me.astype(F32), meta)
    rows[...] = jnp.where(lane < lane_class, mapped, meta)


def pack(target, cost, forcing, level_map, workers, capacity):
    columns = forcing.shape[0]
    return pl.pallas_call(
        functools.partial(pack_kernel, capacity, workers),
        out_shape=jax.ShapeDtypeStruct((columns, LANES), F32),
        in_specs=[pl.BlockSpec(memory_space=pltpu.SMEM)] * 2 + [pl.BlockSpec(memory_space=pltpu.VMEM)] * 2,
        out_specs=pl.BlockSpec(memory_space=pltpu.VMEM),
        scratch_shapes=[pltpu.SMEM((workers,), jnp.int32)],
        name="pack_forcing",
    )(target, cost, forcing, level_map)


def model_kernel(workers, slots, levels, width, *refs):
    row_refs = refs[:workers]
    x_hbm = refs[workers]
    y_hbm, t_ref = refs[workers + 1 : workers + 3]
    cloud_hbm = refs[workers + 3 : 2 * workers + 3]
    (xs, cl, nat, s0, s1, saved, coef, rows_s, meta_v, meta_s, sem_meta, sem_in, sem_out, sem_cloud) = refs[2 * workers + 3 :]
    groups = xs.shape[1] // ROWS
    padded = groups * ROWS
    capacity = slots // workers
    tiles = levels * width // LANES
    residues = width // ROWS
    lane_class, lane_slot, lane_column, lane_owner = lanes_of(levels)
    me = lax.axis_index("crm")

    rows = jnp.concatenate([ref[...] for ref in row_refs], axis=0)
    lane_c = iota(rows.shape, 1)
    local = rows[:, lane_slot : lane_slot + 1] - (me * slots).astype(F32)
    member = (local == lane_c.astype(F32)) & (lane_c < slots)
    class_row = jnp.sum(jnp.where(member, rows[:, lane_class : lane_class + 1], 0.0), axis=0, keepdims=True)
    sub_p = iota((padded, LANES), 0)
    lane_p = iota((padded, LANES), 1)
    key_row = class_row * LANES + (LANES - 1 - iota((1, LANES), 1)).astype(F32)
    key_col = jnp.sum(jnp.where(sub_p == lane_p, key_row, 0.0), axis=1, keepdims=True)
    class_col = jnp.sum(jnp.where(sub_p == lane_p, class_row, 0.0), axis=1, keepdims=True)
    ahead_row = ((key_col > key_row) & (sub_p < slots)).astype(F32)
    place_row = jnp.sum(ahead_row, axis=0, keepdims=True)
    ahead_col = ((key_row > key_col) & (lane_p < slots)).astype(F32)
    place_col = jnp.sum(ahead_col, axis=1, keepdims=True)
    here = (place_col == lane_p.astype(F32)) & (sub_p < slots)
    order = jnp.sum(jnp.where(here, sub_p.astype(F32), 0.0), axis=0, keepdims=True)
    class_sorted = jnp.sum(jnp.where(here, class_col, 0.0), axis=0, keepdims=True)
    sub_m = iota((ROWS, LANES), 0)
    lane_m = iota((ROWS, LANES), 1)
    meta_v[...] = jnp.where(sub_m == 0, order, jnp.where(sub_m == 1, class_sorted, 0.0)).astype(jnp.int32)
    fetch = pltpu.make_async_copy(meta_v, meta_s, sem_meta)
    fetch.start()
    place_of = jnp.sum(jnp.where(member, place_row + 1.0, 0.0), axis=1, keepdims=True) - 1.0
    rows_s[...] = dot_t((place_of == lane_c.astype(F32)).astype(F32), rows)[:padded]
    fetch.wait()

    def load(index, carry):
        slot = meta_s[0, index]
        pltpu.make_async_copy(x_hbm.at[:, pl.ds(slot, 1), :], xs.at[:, pl.ds(index, 1), :], sem_in.at[index]).start()
        return carry

    lax.fori_loop(0, slots, load, 0)

    model_of = lax.rem(lane_m, ROWS)
    step_of = lane_m // ROWS
    own = model_of == sub_m

    def coef_index(name, phase=0):
        names = ("a", "bx", "c0", "c1", "aw", "ac")
        return names.index(name) if name in names else len(names) + ("fh", "fq", "fs").index(name) * PHASES + phase

    def at(field, phase, residue):
        return (field * PHASES + phase) * residues + residue

    def substep(src, dst):
        def self_at(field, phase, residue):
            return src[at(field, phase, residue)]

        def above(field, phase, residue):
            if phase < PHASES - 1:
                return src[at(field, phase + 1, residue)]
            return pltpu.roll(src[at(field, 0, residue)], LANES - ROWS, 1)

        def below(field, phase, residue):
            if phase > 0:
                return src[at(field, phase - 1, residue)]
            return pltpu.roll(src[at(field, PHASES - 1, residue)], ROWS, 1)

        a, bx, aw, ac = (coef[coef_index(name)] for name in ("a", "bx", "aw", "ac"))
        for phase in range(PHASES):
            c1 = coef[coef_index("c0" if phase < 2 else "c1")]
            fh, fq, fs = (coef[coef_index(name, phase)] for name in ("fh", "fq", "fs"))
            first = [self_at(field, phase, 0) for field in range(3)]
            left = [pltpu.roll(self_at(field, phase, residues - 1), 1, 0) for field in range(3)]
            here = first
            pushed = []
            for residue in range(residues):
                if residue < residues - 1:
                    right = [self_at(field, phase, residue + 1) for field in range(3)]
                else:
                    right = [pltpu.roll(first[field], ROWS - 1, 0) for field in range(3)]
                heat, moist, wind = here
                up_coef = c1 - wind
                down_coef = c1 + wind
                new_heat = (a * heat + fh) + bx * (left[0] + right[0])
                new_heat = new_heat + (up_coef * above(0, phase, residue) + down_coef * below(0, phase, residue))
                new_moist = jnp.minimum(a * moist + fq, ac * moist + fs) + bx * (left[1] + right[1])
                new_moist = new_moist + (up_coef * above(1, phase, residue) + down_coef * below(1, phase, residue))
                new_wind = (aw * wind + (heat - moist)) + bx * (left[2] + right[2])
                new_wind = new_wind + c1 * (above(2, phase, residue) + below(2, phase, residue))
                dst[at(0, phase, residue)] = new_heat
                dst[at(1, phase, residue)] = new_moist
                pushed.append(new_wind)
                left, here = here, right
            total = pushed
            while len(total) > 1:
                total = [sum(total[i : i + 2]) for i in range(0, len(total), 2)]
            mean = all_rows(total[0]) * (1.0 / width)
            for residue in range(residues):
                dst[at(2, phase, residue)] = pushed[residue] - mean

    def run_group(group, carry):
        base = pl.multiple_of(group * ROWS, ROWS)
        units = meta_s[1, base]
        mixed = meta_s[1, base + ROWS - 1] != units

        def wait_in(member_index, inner):
            index = base + member_index

            @pl.when(index < slots)
            def _():
                pltpu.make_async_copy(x_hbm.at[:, pl.ds(0, 1), :], xs.at[:, pl.ds(index, 1), :], sem_in.at[index]).wait()

            return inner

        lax.fori_loop(0, ROWS, wait_in, 0)

        @pl.when(units > 0)
        def _():
            mine = rows_s[pl.ds(base, ROWS), :]
            class_m = mine[:, lane_class : lane_class + 1]
            class_l = all_rows(jnp.where(own, class_m, 0.0))
            steps = jnp.maximum(class_l * SUB, 1.0)
            dt = 1.0 / steps
            scale = 0.5 * dt * dt
            moist_weight = 1.0 - MOIST_BUOYANCY
            diffuse = 1.0 - 2.0 * (DIFFUSE_HORIZ + DIFFUSE_VERT) * dt
            coef[coef_index("a")] = diffuse
            coef[coef_index("bx")] = DIFFUSE_HORIZ * dt
            inside = [(PHASES * step_of + phase) < levels for phase in range(PHASES)]
            coef[coef_index("c0")] = jnp.where(inside[1], DIFFUSE_VERT * dt, 0.0)
            coef[coef_index("c1")] = jnp.where(inside[3], DIFFUSE_VERT * dt, 0.0)
            coef[coef_index("aw")] = diffuse - LINEAR_DRAG * dt
            coef[coef_index("ac")] = diffuse - CONDENSE_RATE * dt
            for phase in range(PHASES):
                level = PHASES * step_of + phase
                pick = jnp.minimum(level, levels - 1)
                keep = own & inside[phase]
                force = [
                    all_rows(jnp.where(keep, jnp.take_along_axis(mine, pick + variable * levels, axis=1), 0.0))
                    for variable in range(2)
                ]
                saturated = jnp.where(inside[phase], 1.0 - 2.0 * (level.astype(F32) + 0.5) / levels, 0.0)
                fq = (moist_weight * scale * dt) * force[1]
                coef[coef_index("fh", phase)] = (scale * dt) * (force[0] + force[1])
                coef[coef_index("fq", phase)] = fq
                coef[coef_index("fs", phase)] = fq + (CONDENSE_RATE * moist_weight) * dt * scale * saturated

            zero = jnp.zeros((ROWS, LANES), F32)
            for field in range(3):
                for half in range(2):
                    parts = []
                    for step in range(LANES // ROWS):
                        tile = 2 * step + half
                        parts.append(xs[field, pl.ds(base, ROWS), tile * LANES : (tile + 1) * LANES] if tile < tiles else zero)
                    start = (field * PHASES + 2 * half) * width
                    nat[start : start + LANES, :] = jnp.concatenate(parts, axis=0).T

            def natural(field, phase, residue):
                return pl.ds((field * PHASES + phase) * width + residue, ROWS, stride=residues)

            moist_scale = moist_weight * scale
            wind_scale = 0.5 * dt
            for phase in range(PHASES):
                for residue in range(residues):
                    theta, moist, wind = (nat[natural(field, phase, residue), :] for field in range(3))
                    s0[at(0, phase, residue)] = scale * (theta + moist)
                    s0[at(1, phase, residue)] = moist_scale * moist
                    s0[at(2, phase, residue)] = wind_scale * wind

            def unit(index, inner):
                for _ in range(SUB // 2):
                    substep(s0, s1)
                    substep(s1, s0)

                @pl.when(mixed & (index + 1 < units))
                def _():
                    done = class_l == (index + 1).astype(F32)
                    for entry in range(3 * PHASES * residues):
                        saved[entry] = jnp.where(done, s0[entry], saved[entry])

                return inner

            lax.fori_loop(0, units, unit, 0)

            last = class_l == units.astype(F32)
            inv_scale = 2.0 * steps * steps
            inv_moist = inv_scale * (1.0 / moist_weight)
            inv_wind = 2.0 * steps
            change = []
            for phase in range(PHASES):
                sums = [jnp.zeros((ROWS, LANES), F32)] * 2
                for residue in range(residues):
                    heat, moist, wind = (
                        jnp.where(last, s0[at(field, phase, residue)], saved[at(field, phase, residue)]) for field in range(3)
                    )
                    moist = inv_moist * moist
                    theta = inv_scale * heat - moist
                    for variable, value in enumerate((theta, moist)):
                        sums[variable] = sums[variable] + (value - nat[natural(variable, phase, residue), :])
                    for field, value in enumerate((theta, moist, inv_wind * wind)):
                        nat[natural(field, phase, residue), :] = value
                change.append([all_rows(value) * (1.0 / width) for value in sums])

            active = class_m > 0.0
            second = lane_m >= levels
            level = jnp.where(second, lane_m - levels, lane_m)
            pick = jnp.minimum(level // PHASES * ROWS + sub_m, LANES - 1)
            which = lax.rem(level, PHASES)
            tendency = jnp.zeros((ROWS, LANES), F32)
            for phase in range(PHASES):
                found = [jnp.take_along_axis(change[phase][variable], pick, axis=1) for variable in range(2)]
                tendency = jnp.where(which == phase, jnp.where(second, found[1], found[0]), tendency)
            t_ref[pl.ds(base, ROWS), :] = jnp.where((lane_m < lane_class) & active, tendency, jnp.where(lane_m < lane_class, 0.0, mine))

            for field in range(3):
                for half in range(2):
                    start = (field * PHASES + 2 * half) * width
                    back = nat[start : start + LANES, :].T
                    for step in range(LANES // ROWS):
                        tile = 2 * step + half
                        if tile >= tiles:
                            continue
                        spot = (field, pl.ds(base, ROWS), slice(tile * LANES, (tile + 1) * LANES))
                        value = back[step * ROWS : (step + 1) * ROWS]
                        xs[spot] = jnp.where(active, value, xs[spot])
                        if field == 1:
                            level = (LANES // width) * tile + lane_m // width
                            saturated = 1.0 - 2.0 * (level.astype(F32) + 0.5) / levels
                            cl[pl.ds(base, ROWS), tile * LANES : (tile + 1) * LANES] = jnp.maximum(value - saturated, 0.0)

        @pl.when(units <= 0)
        def _():
            t_ref[pl.ds(base, ROWS), :] = jnp.zeros((ROWS, LANES), F32)

        def store(member_index, inner):
            index = base + member_index

            @pl.when(index < slots)
            def _():
                slot = meta_s[0, index]
                pltpu.make_async_copy(xs.at[:, pl.ds(index, 1), :], y_hbm.at[:, pl.ds(slot, 1), :], sem_out.at[index]).start()

                @pl.when(meta_s[1, index] > 0)
                def _():
                    owner = lax.div(slot, capacity)
                    rank = slot - owner * capacity
                    for distance in range(workers):

                        @pl.when(owner == (me ^ distance))
                        def _():
                            pltpu.make_async_copy(
                                cl.at[pl.ds(index, 1), :], cloud_hbm[distance].at[pl.ds(rank, 1), :], sem_cloud.at[index]
                            ).start()

            return inner

        lax.fori_loop(0, ROWS, store, 0)
        return carry

    lax.fori_loop(0, groups, run_group, 0)

    def finish(index, carry):
        pltpu.make_async_copy(xs.at[:, pl.ds(index, 1), :], y_hbm.at[:, pl.ds(0, 1), :], sem_out.at[index]).wait()

        @pl.when(meta_s[1, index] > 0)
        def _():
            pltpu.make_async_copy(cl.at[pl.ds(index, 1), :], cloud_hbm[0].at[pl.ds(0, 1), :], sem_cloud.at[index]).wait()

        return carry

    lax.fori_loop(0, slots, finish, 0)


def run_models(row_blocks, state, levels):
    workers = len(row_blocks)
    _, slots, cells = state.shape
    capacity = slots // workers
    width = cells // levels
    groups = -(-slots // ROWS)
    padded = groups * ROWS
    vmem = pl.BlockSpec(memory_space=pltpu.VMEM)
    hbm = pl.BlockSpec(memory_space=pl.ANY)
    entries = 3 * PHASES * (width // ROWS)
    outs = pl.pallas_call(
        functools.partial(model_kernel, workers, slots, levels, width),
        out_shape=[jax.ShapeDtypeStruct(state.shape, F32), jax.ShapeDtypeStruct((padded, LANES), F32)]
        + [jax.ShapeDtypeStruct((capacity, cells), F32)] * workers,
        in_specs=[vmem] * workers + [hbm],
        out_specs=[hbm, vmem] + [hbm] * workers,
        scratch_shapes=[
            pltpu.VMEM((3, padded, cells), F32),
            pltpu.VMEM((padded, cells), F32),
            pltpu.VMEM((3 * PHASES * width, LANES), F32),
            pltpu.VMEM((entries, ROWS, LANES), F32),
            pltpu.VMEM((entries, ROWS, LANES), F32),
            pltpu.VMEM((entries, ROWS, LANES), F32),
            pltpu.VMEM((6 + 3 * PHASES, ROWS, LANES), F32),
            pltpu.VMEM((padded, LANES), F32),
            pltpu.VMEM((ROWS, LANES), jnp.int32),
            pltpu.SMEM((ROWS, LANES), jnp.int32),
            pltpu.SemaphoreType.DMA,
            pltpu.SemaphoreType.DMA((slots,)),
            pltpu.SemaphoreType.DMA((slots,)),
            pltpu.SemaphoreType.DMA((slots,)),
        ],
        compiler_params=pltpu.CompilerParams(vmem_limit_bytes=24 * MIB),
        name="cloud_models",
    )(*row_blocks, state)
    return outs[0], outs[1], outs[2:]


def edge_kernel(levels, columns, workers, *refs):
    t_refs, out = refs[:workers], refs[workers]
    _, _, lane_column, lane_owner = lanes_of(levels)
    me = lax.axis_index("crm")
    wanted = jnp.where(me == 0, workers - 1, 0).astype(F32)
    rows = jnp.concatenate([ref[...] for ref in t_refs], axis=0)
    lane = iota(rows.shape, 1).astype(F32)
    owner = rows[:, lane_owner : lane_owner + 1]
    column = rows[:, lane_column : lane_column + 1]
    select = ((owner == wanted) & (column == lane + 1.0)).astype(F32)
    out[...] = dot_t(select, rows)[:columns]


def physics_kernel(levels, columns, workers, *refs):
    t_refs = refs[:workers]
    edge, index, weight, level_map, out = refs[workers:]
    _, _, lane_column, lane_owner = lanes_of(levels)
    sources = index.shape[0]
    me = lax.axis_index("crm")
    rows = jnp.concatenate([ref[...] for ref in t_refs], axis=0)
    owner = rows[:, lane_owner : lane_owner + 1]
    column = rows[:, lane_column : lane_column + 1]
    block = owner - me.astype(F32) + 1.0
    named = (column > 0.0) & (block >= 0.0) & (block <= 2.0)
    ident = jnp.where(named, block * columns + column - 1.0, -1.0)
    edge_sub = iota((columns, 1), 0)
    edge_block = jnp.where(me == 0, 0, jnp.where(me == workers - 1, 2, -3))
    edge_ident = (edge_block * columns + edge_sub).astype(F32)
    index_rows = index[...].astype(F32)
    weight_rows = weight[...]
    total = jnp.sum(weight_rows, axis=0, keepdims=True)
    inner = jnp.zeros((rows.shape[0], columns), F32)
    outer = jnp.zeros((columns, columns), F32)
    for source in range(sources):
        wanted = index_rows[source : source + 1]
        share = weight_rows[source : source + 1] / total
        inner = inner + jnp.where(ident == wanted, share, 0.0)
        outer = outer + jnp.where(edge_ident == wanted, share, 0.0)
    edge_rows = jnp.where(edge_block >= 0, edge[...], 0.0)
    mixed = dot_t(inner, rows) + dot_t(outer, edge_rows)
    spread_row = iota((levels, LANES), 0)
    spread_lane = iota((levels, LANES), 1)
    for variable in range(2):
        place = (spread_lane == spread_row + variable * levels).astype(F32)
        out[:, variable, :] = dot(mixed, dot_t(place, level_map[...]))


def cloud_kernel(columns, workers, *refs):
    target = refs[0]
    received = refs[1 : workers + 1]
    out, counts, sem = refs[workers + 1 :]
    me = lax.axis_index("crm")
    for worker in range(workers):
        counts[worker] = 0

    def start(column, carry):
        worker = target[column]
        rank = counts[worker]
        counts[worker] = rank + 1
        for distance in range(workers):

            @pl.when(worker == (me ^ distance))
            def _():
                pltpu.make_async_copy(
                    received[distance].at[pl.ds(rank, 1), :], out.at[pl.ds(column, 1), :], sem.at[column]
                ).start()

        return carry

    lax.fori_loop(0, columns, start, 0)

    def finish(column, carry):
        pltpu.make_async_copy(received[0].at[pl.ds(0, 1), :], out.at[pl.ds(column, 1), :], sem.at[column]).wait()
        return carry

    lax.fori_loop(0, columns, finish, 0)


def exchange(blocks, axis):
    size = lax.axis_size(axis)
    out = [blocks[0]]
    for distance in range(1, size):
        out.append(lax.ppermute(blocks[distance], axis, [(i, i ^ distance) for i in range(size)]))
    return out


def body(crm_state, forcing, target, cost_class, level_map, remap_index, remap_weight):
    workers = lax.axis_size("crm")
    groups = lax.axis_size("grp")
    columns = forcing.shape[0]
    slots, _, cells = crm_state.shape
    capacity = slots // workers
    levels, gcm = level_map.shape
    vmem = pl.BlockSpec(memory_space=pltpu.VMEM)
    hbm = pl.BlockSpec(memory_space=pl.ANY)

    rows = pack(target, cost_class, forcing, level_map, workers, capacity)
    row_blocks = exchange([rows] * workers, "crm")
    state, tendency, clouds = run_models(row_blocks, crm_state.transpose(1, 0, 2), levels)
    tendencies = exchange([tendency] * workers, "crm")

    edge = pl.pallas_call(
        functools.partial(edge_kernel, levels, columns, workers),
        out_shape=jax.ShapeDtypeStruct((columns, LANES), F32),
        in_specs=[vmem] * workers,
        out_specs=vmem,
        name="edge_columns",
    )(*tendencies)
    pairs = []
    for group in range(groups):
        after = (group + 1) % groups
        pairs.append((group * workers, after * workers))
        pairs.append((after * workers + workers - 1, group * workers + workers - 1))
    edge = lax.ppermute(edge, ("grp", "crm"), pairs)
    clouds = exchange(clouds, "crm")
    cloud_water = pl.pallas_call(
        functools.partial(cloud_kernel, columns, workers),
        out_shape=jax.ShapeDtypeStruct((columns, cells), F32),
        in_specs=[pl.BlockSpec(memory_space=pltpu.SMEM)] + [hbm] * workers,
        out_specs=hbm,
        scratch_shapes=[pltpu.SMEM((workers,), jnp.int32), pltpu.SemaphoreType.DMA((columns,))],
        name="cloud_rows",
    )(target, *clouds)
    physics = pl.pallas_call(
        functools.partial(physics_kernel, levels, columns, workers),
        out_shape=jax.ShapeDtypeStruct((columns, 2, gcm), F32),
        in_specs=[vmem] * (workers + 4),
        out_specs=vmem,
        name="physics_cells",
    )(*tendencies, edge, remap_index.T, remap_weight.T, level_map)
    return state.transpose(1, 0, 2), cloud_water, physics


def solution(mesh):
    wide = P(("grp", "crm"), None, None)
    flat = P(("grp", "crm"), None)
    line = P(("grp", "crm"))
    in_specs = (wide, wide, line, line, P(), flat, flat)
    out_specs = (wide, flat, wide)
    return jax.shard_map(body, mesh=mesh, in_specs=in_specs, out_specs=out_specs, check_vma=False)
```

time: 272 us -> 69.8 us (0.26)
  local copies, waits for them, and re-layouts: 100 us -> 5.46 us
  matrix products: 83.1 us -> 0 us
  other arithmetic: 52.3 us -> 0 us
  Pallas kernels: 0 us -> 30.9 us
  waiting for transfers between devices: 11.1 us -> 17.1 us
  starting transfers between devices: 20.5 us -> 14.9 us
    slice x145 -> x0, local copies, waits for them, and re-layouts: 88.5 us -> none  [the longest x48 34 us: horizontal_lap(): jnp.roll(field, -1, -1)]
    dot_general x55 -> x0, matrix products: 83.1 us -> none  [the longest x24 39.2 us: level_mean(): return jnp.dot(means, tables['spreader'], precision=HIGHEST)]
    select_n x26 -> x0, other arithmetic: 48.1 us -> none  [the longest x24 47.4 us: advance(): jnp.where(live, new_field, old_field)]
    pallas_call x0 -> x5, Pallas kernels: none -> 30.9 us  [the longest x1 12.8 us: body(): pl.pallas_call(functools.partial(cloud_kernel, columns, workers), out_sha...]
    ppermute x2 -> x10, waiting for transfers between devices: 0.23 us -> 17.1 us  [the longest x9 12.5 us: exchange(): lax.ppermute(blocks[distance], axis, [(i, i ^ distance) for i in range(si...]
    all_to_all x4 -> x0, starting transfers between devices: 14.3 us -> none  [the longest x1 4.24 us: body(): lax.all_to_all(send_class.reshape(workers, capacity), 'crm', split_axis=0...]
    all_to_all x4 -> x0, waiting for transfers between devices: 10.8 us -> none  [the longest x1 4.24 us: body(): lax.all_to_all(condensate.reshape(workers, capacity, cell_count), 'crm',...]
    ppermute x2 -> x10, starting transfers between devices: 6.22 us -> 14.9 us  [the longest x9 11 us: exchange(): lax.ppermute(blocks[distance], axis, [(i, i ^ distance) for i in range(si...]
  transfers between devices with their start and end apart: 6 -> 10, of which waited for: 4 -> 5; matrix products, arithmetic and copies ran while one was open for 3% -> 0% of each run, Pallas kernels for 0% -> 6%
where the time goes in v1:
time: 69.8 us; the launch traced here: 69.1 us
  Pallas kernels  30.9 us (44%)
  waiting for transfers between devices  17.1 us (24%)
  starting transfers between devices  14.9 us (21%)
  local copies, waits for them, and re-layouts  5.46 us (8%)
  between operations  0.7 us (1%)
    pallas_call x1, Pallas kernels, body(): pl.pallas_call(functools.partial(cloud_kernel, columns, workers), out_sha...  12.8 us
    ppermute x9, waiting for transfers between devices, exchange(): lax.ppermute(blocks[distance], axis, [(i, i ^ distance) for i in range(si...  12.5 us
    pallas_call x1, Pallas kernels, run_models(): pl.pallas_call(functools.partial(model_kernel, workers, slots, levels, wi...  12 us
    ppermute x9, starting transfers between devices, exchange(): lax.ppermute(blocks[distance], axis, [(i, i ^ distance) for i in range(si...  11 us
    unnamed x22, local copies, waits for them, and re-layouts  5.46 us
    ppermute x1, waiting for transfers between devices, body(): edge = lax.ppermute(edge, ('grp', 'crm'), pairs)  4.65 us
    ppermute x1, starting transfers between devices, body(): edge = lax.ppermute(edge, ('grp', 'crm'), pairs)  3.82 us
    pallas_call x1, Pallas kernels, body(): pl.pallas_call(functools.partial(physics_kernel, levels, columns, workers...  2.34 us
  transfers between devices with their start and end apart: 10, of which 5 were waited for; matrix products, arithmetic and copies ran while one was open for 0% of the time, Pallas kernels for 6%

profile of v1, /device:TPU:0, one launch (start us, length us, event | category | flops | bytes accessed | tf_op | source)
XLA Modules:
  0.0 69.1 jit_solution(6154832873827812771)
XLA Ops:
  0.6 2.0 %pack_forcing.1.refs_0_ = f32[24,128]{1,0:T(8,128)} custom-call(s32[24]{0:T(128)} %refs_0_.1, s32[24]{0:T(128)} %cost.1, f32[24,2,72]{2,1,0:T(2,128)} %forcing.1, f32[58,72]{1,0:T(8,128)} %refs_7_.1), custom_call_target="tpu_custom_call" | custom-call | tf_op jit(solution)/shard_map/pack_forcing/pallas_call | solution.py:81
  2.6 0.5 collective-permute-start
  3.1 2.5 %collective-permute-start.1 = (f32[24,128]{1,0:T(8,128)}, f32[24,128]{1,0:T(8,128)S(1)}, u32[]{:S(2)}, u32[]{:S(2)}) collective-permute-start(f32[24,128]{1,0:T(8,128)} %pack_forcing.1.refs_0_), channel_id=1, source_target_pairs={{0,2},{1,3},{2,0},{3,1},{4,6},{5,7},{6,4},{7,5},{8,10},{9,11},{10,... | collective-permute-start | bytes 36872 | tf_op jit(solution)/shard_map/ppermute | solution.py:489
  5.6 0.1 collective-permute-start.2
  5.7 0.0 collective-permute-done.refs_1_
  5.7 1.7 %collective-permute-done.1.refs_2_ = f32[24,128]{1,0:T(8,128)S(1)} collective-permute-done((f32[24,128]{1,0:T(8,128)}, f32[24,128]{1,0:T(8,128)S(1)}, u32[]{:S(2)}, u32[]{:S(2)}) %collective-permute-start.1) | collective-permute-done | bytes 12320 | tf_op jit(solution)/shard_map/ppermute | solution.py:489
  7.5 1.4 %collective-permute-done.2.refs_3_ = f32[24,128]{1,0:T(8,128)S(1)} collective-permute-done((f32[24,128]{1,0:T(8,128)}, f32[24,128]{1,0:T(8,128)S(1)}, u32[]{:S(2)}, u32[]{:S(2)}) %collective-permute-start.2) | collective-permute-done | bytes 12320 | tf_op jit(solution)/shard_map/ppermute | solution.py:489
  8.9 0.0 copy-start
  8.9 1.5 %copy-done = f32[36,3,3712]{2,0,1:T(8,128)S(1)} copy-done((f32[36,3,3712]{2,0,1:T(8,128)S(1)}, f32[36,3,3712]{2,0,1:T(8,128)}, u32[]{:S(2)}) %copy-start) | copy-done | bytes 1603608
  10.4 0.0 copy-start.3
  10.4 0.7 %copy-done.3 = f32[24,128]{1,0:T(8,128)S(1)} copy-done((f32[24,128]{1,0:T(8,128)S(1)}, f32[24,128]{1,0:T(8,128)}, u32[]{:S(2)}) %copy-start.3) | copy-done | bytes 12312
  11.1 12.0 %cloud_models.1 = (f32[3,36,3712]{2,1,0:T(8,128)}, f32[40,128]{1,0:T(8,128)S(1)}, f32[9,3712]{1,0:T(8,128)S(1)}, f32[9,3712]{1,0:T(8,128)S(1)}, f32[9,3712]{1,0:T(8,128)S(1)}, /*index=5*/f32[9,3712]{1,0:T(8,128)S(1)}) custom-call(f32[24,128]{1,0:T(8,128)S(1)} %copy-done.3, f32[24,128]{1,0:T(8,128)S(1)} %collective-permute-done.refs_1_, ...), custom_call_target="tpu_custom_call" | custom-call | tf_op jit(solution)/shard_map/cloud_models/pallas_call | solution.py:379
  23.1 0.0 copy-start.1
  23.1 0.7 copy-done.1
  23.8 0.0 copy-start.2
  23.8 1.7 %collective-permute-start.3 = (f32[9,3712]{1,0:T(8,128)S(1)}, f32[9,3712]{1,0:T(8,128)S(1)}, u32[]{:S(2)}, u32[]{:S(2)}) collective-permute-start(f32[9,3712]{1,0:T(8,128)S(1)} %get-tuple-element.11), channel_id=1, source_target_pairs={{0,1},{1,0},{2,3},{3,2},{4,5},{5,4},{6,7},{7,6},{8,9},{9,8},{10,11... | collective-permute-start | bytes 400904 | tf_op jit(solution)/shard_map/ppermute | solution.py:489
  25.6 3.3 %collective-permute-start.4 = (f32[9,3712]{1,0:T(8,128)S(1)}, f32[9,3712]{1,0:T(8,128)S(1)}, u32[]{:S(2)}, u32[]{:S(2)}) collective-permute-start(f32[9,3712]{1,0:T(8,128)S(1)} %get-tuple-element.12), channel_id=1, source_target_pairs={{0,2},{1,3},{2,0},{3,1},{4,6},{5,7},{6,4},{7,5},{8,10},{9,11},{10,... | collective-permute-start | bytes 400904 | tf_op jit(solution)/shard_map/ppermute | solution.py:489
  28.8 0.1 collective-permute-start.5
  29.0 0.1 collective-permute-start.6
  29.1 1.9 %collective-permute-start.7 = (f32[40,128]{1,0:T(8,128)S(1)}, f32[40,128]{1,0:T(8,128)S(1)}, u32[]{:S(2)}, u32[]{:S(2)}) collective-permute-start(f32[40,128]{1,0:T(8,128)S(1)} %get-tuple-element.14.refs_0_), channel_id=1, source_target_pairs={{0,2},{1,3},{2,0},{3,1},{4,6},{5,7},{6,4},{7,5},{8,10},{9,11},{10,... | collective-permute-start | bytes 61448 | tf_op jit(solution)/shard_map/ppermute | solution.py:489
  31.0 0.0 collective-permute-done.6.refs_1_
  31.0 0.0 copy-start.7
  31.0 0.8 %collective-permute-start.8 = (f32[40,128]{1,0:T(8,128)S(1)}, f32[40,128]{1,0:T(8,128)S(1)}, u32[]{:S(2)}, u32[]{:S(2)}) collective-permute-start(f32[40,128]{1,0:T(8,128)S(1)} %get-tuple-element.14.refs_0_), channel_id=1, source_target_pairs={{0,3},{1,2},{2,1},{3,0},{4,7},{5,6},{6,5},{7,4},{8,11},{9,10},{10,... | collective-permute-start | bytes 61448 | tf_op jit(solution)/shard_map/ppermute | solution.py:489
  31.8 9.2 %collective-permute-done.7.refs_2_ = f32[40,128]{1,0:T(8,128)S(1)} collective-permute-done((f32[40,128]{1,0:T(8,128)S(1)}, f32[40,128]{1,0:T(8,128)S(1)}, u32[]{:S(2)}, u32[]{:S(2)}) %collective-permute-start.7) | collective-permute-done | bytes 20512 | tf_op jit(solution)/shard_map/ppermute | solution.py:489
  41.0 0.0 copy-start.8
  41.0 0.1 collective-permute-done.8.refs_3_
  41.1 0.0 copy-done.2
  41.1 0.0 copy-done.7
  41.1 0.5 copy-done.8
  41.6 0.0 copy-start.9
  41.6 0.6 copy-done.9
  42.2 1.8 %edge_columns.1 = f32[24,128]{1,0:T(8,128)} custom-call(f32[40,128]{1,0:T(8,128)} %copy-done.2, f32[40,128]{1,0:T(8,128)} %copy-done.7, f32[40,128]{1,0:T(8,128)} %copy-done.8, f32[40,128]{1,0:T(8,128)} %copy-done.9), custom_call_target="tpu_custom_call" | custom-call | tf_op jit(solution)/shard_map/edge_columns/pallas_call | solution.py:508
  44.0 3.8 %collective-permute-start.9 = (f32[24,128]{1,0:T(8,128)}, f32[24,128]{1,0:T(8,128)S(1)}, u32[]{:S(2)}, u32[]{:S(2)}) collective-permute-start(f32[24,128]{1,0:T(8,128)} %edge_columns.1), channel_id=1, source_target_pairs={{0,4},{7,3},{4,8},{11,7},{8,12},{15,11},{12,16},{19,15},{16,20},{2... | collective-permute-start | bytes 36872 | tf_op jit(solution)/shard_map/ppermute | solution.py:520
  47.8 4.7 %collective-permute-done.9.refs_4_ = f32[24,128]{1,0:T(8,128)S(1)} collective-permute-done((f32[24,128]{1,0:T(8,128)}, f32[24,128]{1,0:T(8,128)S(1)}, u32[]{:S(2)}, u32[]{:S(2)}) %collective-permute-start.9) | collective-permute-done | bytes 12320 | tf_op jit(solution)/shard_map/ppermute | solution.py:520
  52.4 0.0 copy-start.10
  52.4 0.6 copy-done.10
  53.1 2.3 %physics_cells.1 = f32[24,2,72]{2,1,0:T(2,128)} custom-call(f32[40,128]{1,0:T(8,128)} %copy-done.2, f32[40,128]{1,0:T(8,128)} %copy-done.7, f32[40,128]{1,0:T(8,128)} %copy-done.8, f32[40,128]{1,0:T(8,128)} %copy-done.9, f32[24,128]{1,0:T(8,128)} %copy-done.10, s32[4,24]{1,0:T(4,128)} %bitcast.5, f32[4,24]{1,0:T(4,128)} %bitcast.6, f32[58,72]{1,0:T(8,128)} %refs_7_.1), custom_call_target="tpu_custom_call" | custom-call | tf_op jit(solution)/shard_map/physics_cells/pallas_call | solution.py:530
  55.4 0.0 collective-permute-done.3.refs_2_
  55.4 0.0 copy-start.4
  55.4 0.0 collective-permute-done.4.refs_3_
  55.4 0.0 copy-start.5
  55.4 0.0 collective-permute-done.5.refs_4_
  55.4 0.0 copy-start.6
  55.4 0.6 copy-done.4
  56.1 0.1 copy-done.5
  56.2 0.1 copy-done.6
  56.3 12.8 %cloud_rows.1 = f32[24,3712]{1,0:T(8,128)} custom-call(s32[24]{0:T(128)} %refs_0_.1, f32[9,3712]{1,0:T(8,128)} %copy-done.1, f32[9,3712]{1,0:T(8,128)} %copy-done.4, f32[9,3712]{1,0:T(8,128)} %copy-done.5, f32[9,3712]{1,0:T(8,128)} %copy-done.6), custom_call_target="tpu_custom_call" | custom-call | tf_op jit(solution)/shard_map/cloud_rows/pallas_call | solution.py:522
Async XLA Ops:
  2.6 3.1 %collective-permute-start = (f32[24,128]{1,0:T(8,128)}, f32[24,128]{1,0:T(8,128)S(1)}, u32[]{:S(2)}, u32[]{:S(2)}) collective-permute-start(f32[24,128]{1,0:T(8,128)} %pack_forcing.1.refs_0_), channel_id=1, source_target_pairs={{0,1},{1,0},{2,3},{3,2},{4,5},{5,4},{6,7},{7,6},{8,9},{9,8},{10,11... | collective-permute-start | bytes 36872 | tf_op jit(solution)/shard_map/ppermute | solution.py:489
  3.1 4.4 %collective-permute-start.1 = (f32[24,128]{1,0:T(8,128)}, f32[24,128]{1,0:T(8,128)S(1)}, u32[]{:S(2)}, u32[]{:S(2)}) collective-permute-start(f32[24,128]{1,0:T(8,128)} %pack_forcing.1.refs_0_), channel_id=1, source_target_pairs={{0,2},{1,3},{2,0},{3,1},{4,6},{5,7},{6,4},{7,5},{8,10},{9,11},{10,... | collective-permute-start | bytes 36872 | tf_op jit(solution)/shard_map/ppermute | solution.py:489
  5.6 3.3 %collective-permute-start.2 = (f32[24,128]{1,0:T(8,128)}, f32[24,128]{1,0:T(8,128)S(1)}, u32[]{:S(2)}, u32[]{:S(2)}) collective-permute-start(f32[24,128]{1,0:T(8,128)} %pack_forcing.1.refs_0_), channel_id=1, source_target_pairs={{0,3},{1,2},{2,1},{3,0},{4,7},{5,6},{6,5},{7,4},{8,11},{9,10},{10,... | collective-permute-start | bytes 36872 | tf_op jit(solution)/shard_map/ppermute | solution.py:489
  8.9 1.5 %copy-start = (f32[36,3,3712]{2,0,1:T(8,128)S(1)}, f32[36,3,3712]{2,0,1:T(8,128)}, u32[]{:S(2)}) copy-start(f32[36,3,3712]{2,0,1:T(8,128)} %param.7) | copy-start | bytes 4810756
  10.4 0.7 %copy-start.3 = (f32[24,128]{1,0:T(8,128)S(1)}, f32[24,128]{1,0:T(8,128)}, u32[]{:S(2)}) copy-start(f32[24,128]{1,0:T(8,128)} %pack_forcing.1.refs_0_) | copy-start | bytes 36868
  23.1 0.7 %copy-start.1 = (f32[9,3712]{1,0:T(8,128)}, f32[9,3712]{1,0:T(8,128)S(1)}, u32[]{:S(2)}) copy-start(f32[9,3712]{1,0:T(8,128)S(1)} %get-tuple-element.10.refs_1_) | copy-start | bytes 400900
  23.8 17.2 %copy-start.2 = (f32[40,128]{1,0:T(8,128)}, f32[40,128]{1,0:T(8,128)S(1)}, u32[]{:S(2)}) copy-start(f32[40,128]{1,0:T(8,128)S(1)} %get-tuple-element.14.refs_0_) | copy-start | bytes 61444
  23.8 31.6 %collective-permute-start.3 = (f32[9,3712]{1,0:T(8,128)S(1)}, f32[9,3712]{1,0:T(8,128)S(1)}, u32[]{:S(2)}, u32[]{:S(2)}) collective-permute-start(f32[9,3712]{1,0:T(8,128)S(1)} %get-tuple-element.11), channel_id=1, source_target_pairs={{0,1},{1,0},{2,3},{3,2},{4,5},{5,4},{6,7},{7,6},{8,9},{9,8},{10,11... | collective-permute-start | bytes 400904 | tf_op jit(solution)/shard_map/ppermute | solution.py:489
  25.6 29.8 %collective-permute-start.4 = (f32[9,3712]{1,0:T(8,128)S(1)}, f32[9,3712]{1,0:T(8,128)S(1)}, u32[]{:S(2)}, u32[]{:S(2)}) collective-permute-start(f32[9,3712]{1,0:T(8,128)S(1)} %get-tuple-element.12), channel_id=1, source_target_pairs={{0,2},{1,3},{2,0},{3,1},{4,6},{5,7},{6,4},{7,5},{8,10},{9,11},{10,... | collective-permute-start | bytes 400904 | tf_op jit(solution)/shard_map/ppermute | solution.py:489
  28.8 26.6 %collective-permute-start.5 = (f32[9,3712]{1,0:T(8,128)S(1)}, f32[9,3712]{1,0:T(8,128)S(1)}, u32[]{:S(2)}, u32[]{:S(2)}) collective-permute-start(f32[9,3712]{1,0:T(8,128)S(1)} %get-tuple-element.13), channel_id=1, source_target_pairs={{0,3},{1,2},{2,1},{3,0},{4,7},{5,6},{6,5},{7,4},{8,11},{9,10},{10,... | collective-permute-start | bytes 400904 | tf_op jit(solution)/shard_map/ppermute | solution.py:489
  29.0 2.0 %collective-permute-start.6 = (f32[40,128]{1,0:T(8,128)S(1)}, f32[40,128]{1,0:T(8,128)S(1)}, u32[]{:S(2)}, u32[]{:S(2)}) collective-permute-start(f32[40,128]{1,0:T(8,128)S(1)} %get-tuple-element.14.refs_0_), channel_id=1, source_target_pairs={{0,1},{1,0},{2,3},{3,2},{4,5},{5,4},{6,7},{7,6},{8,9},{9,8},{10,11... | collective-permute-start | bytes 61448 | tf_op jit(solution)/shard_map/ppermute | solution.py:489
  29.1 11.9 %collective-permute-start.7 = (f32[40,128]{1,0:T(8,128)S(1)}, f32[40,128]{1,0:T(8,128)S(1)}, u32[]{:S(2)}, u32[]{:S(2)}) collective-permute-start(f32[40,128]{1,0:T(8,128)S(1)} %get-tuple-element.14.refs_0_), channel_id=1, source_target_pairs={{0,2},{1,3},{2,0},{3,1},{4,6},{5,7},{6,4},{7,5},{8,10},{9,11},{10,... | collective-permute-start | bytes 61448 | tf_op jit(solution)/shard_map/ppermute | solution.py:489
  31.0 10.1 %copy-start.7 = (f32[40,128]{1,0:T(8,128)}, f32[40,128]{1,0:T(8,128)S(1)}, u32[]{:S(2)}) copy-start(f32[40,128]{1,0:T(8,128)S(1)} %collective-permute-done.6.refs_1_) | copy-start | bytes 61444
  31.0 10.1 %collective-permute-start.8 = (f32[40,128]{1,0:T(8,128)S(1)}, f32[40,128]{1,0:T(8,128)S(1)}, u32[]{:S(2)}, u32[]{:S(2)}) collective-permute-start(f32[40,128]{1,0:T(8,128)S(1)} %get-tuple-element.14.refs_0_), channel_id=1, source_target_pairs={{0,3},{1,2},{2,1},{3,0},{4,7},{5,6},{6,5},{7,4},{8,11},{9,10},{10,... | collective-permute-start | bytes 61448 | tf_op jit(solution)/shard_map/ppermute | solution.py:489
  41.0 0.6 copy-start.8
  41.6 0.6 copy-start.9
  44.0 8.5 %collective-permute-start.9 = (f32[24,128]{1,0:T(8,128)}, f32[24,128]{1,0:T(8,128)S(1)}, u32[]{:S(2)}, u32[]{:S(2)}) collective-permute-start(f32[24,128]{1,0:T(8,128)} %edge_columns.1), channel_id=1, source_target_pairs={{0,4},{7,3},{4,8},{11,7},{8,12},{15,11},{12,16},{19,15},{16,20},{2... | collective-permute-start | bytes 36872 | tf_op jit(solution)/shard_map/ppermute | solution.py:520
  52.4 0.6 copy-start.10
  55.4 0.7 copy-start.4
  55.4 0.8 %copy-start.5 = (f32[9,3712]{1,0:T(8,128)}, f32[9,3712]{1,0:T(8,128)S(1)}, u32[]{:S(2)}) copy-start(f32[9,3712]{1,0:T(8,128)S(1)} %collective-permute-done.4.refs_3_) | copy-start | bytes 400900
  55.4 0.9 %copy-start.6 = (f32[9,3712]{1,0:T(8,128)}, f32[9,3712]{1,0:T(8,128)S(1)}, u32[]{:S(2)}) copy-start(f32[9,3712]{1,0:T(8,128)S(1)} %collective-permute-done.5.refs_4_) | copy-start | bytes 400900

commit v2 on v1

--- a/solution.py
+++ b/solution.py
@@ -84,6 +84,7 @@
         in_specs=[pl.BlockSpec(memory_space=pltpu.SMEM)] * 2 + [pl.BlockSpec(memory_space=pltpu.VMEM)] * 2,
         out_specs=pl.BlockSpec(memory_space=pltpu.VMEM),
         scratch_shapes=[pltpu.SMEM((workers,), jnp.int32)],
+        compiler_params=pltpu.CompilerParams(vmem_limit_bytes=8 * MIB),
         name="pack_forcing",
     )(target, cost, forcing, level_map)
 
@@ -121,7 +122,11 @@
     class_sorted = jnp.sum(jnp.where(here, class_col, 0.0), axis=0, keepdims=True)
     sub_m = iota((ROWS, LANES), 0)
     lane_m = iota((ROWS, LANES), 1)
-    meta_v[...] = jnp.where(sub_m == 0, order, jnp.where(sub_m == 1, class_sorted, 0.0)).astype(jnp.int32)
+    owner_row = jnp.floor((order + 0.5) * (1.0 / capacity))
+    rank_row = order - owner_row * capacity
+    away_row = owner_row.astype(jnp.int32) ^ me
+    table = jnp.where(sub_m == 0, order, jnp.where(sub_m == 1, class_sorted, rank_row)).astype(jnp.int32)
+    meta_v[...] = jnp.where(sub_m == 2, away_row, table)
     fetch = pltpu.make_async_copy(meta_v, meta_s, sem_meta)
     fetch.start()
     place_of = jnp.sum(jnp.where(member, place_row + 1.0, 0.0), axis=1, keepdims=True) - 1.0
@@ -130,10 +135,11 @@
 
     def load(index, carry):
         slot = meta_s[0, index]
-        pltpu.make_async_copy(x_hbm.at[:, pl.ds(slot, 1), :], xs.at[:, pl.ds(index, 1), :], sem_in.at[index]).start()
+        group = lax.shift_right_logical(index, 3)
+        pltpu.make_async_copy(x_hbm.at[:, pl.ds(slot, 1), :], xs.at[:, pl.ds(index, 1), :], sem_in.at[group]).start()
         return carry
 
-    lax.fori_loop(0, slots, load, 0)
+    lax.fori_loop(0, padded, load, 0, unroll=4)
 
     model_of = lax.rem(lane_m, ROWS)
     step_of = lane_m // ROWS
@@ -198,16 +204,8 @@
         units = meta_s[1, base]
         mixed = meta_s[1, base + ROWS - 1] != units
 
-        def wait_in(member_index, inner):
-            index = base + member_index
-
-            @pl.when(index < slots)
-            def _():
-                pltpu.make_async_copy(x_hbm.at[:, pl.ds(0, 1), :], xs.at[:, pl.ds(index, 1), :], sem_in.at[index]).wait()
-
-            return inner
-
-        lax.fori_loop(0, ROWS, wait_in, 0)
+        here = xs.at[:, pl.ds(base, ROWS), :]
+        pltpu.make_async_copy(here, here, sem_in.at[group]).wait()
 
         @pl.when(units > 0)
         def _():
@@ -327,43 +325,32 @@
         def _():
             t_ref[pl.ds(base, ROWS), :] = jnp.zeros((ROWS, LANES), F32)
 
-        def store(member_index, inner):
-            index = base + member_index
-
-            @pl.when(index < slots)
-            def _():
-                slot = meta_s[0, index]
-                pltpu.make_async_copy(xs.at[:, pl.ds(index, 1), :], y_hbm.at[:, pl.ds(slot, 1), :], sem_out.at[index]).start()
-
-                @pl.when(meta_s[1, index] > 0)
+        def store(member):
+            index = base + member
+            slot = meta_s[0, index]
+            rank = meta_s[3, index]
+            away = meta_s[2, index]
+            pltpu.make_async_copy(xs.at[:, pl.ds(index, 1), :], y_hbm.at[:, pl.ds(slot, 1), :], sem_out.at[index]).start()
+            for distance in range(workers):
+
+                @pl.when(away == distance)
                 def _():
-                    owner = lax.div(slot, capacity)
-                    rank = slot - owner * capacity
-                    for distance in range(workers):
-
-                        @pl.when(owner == (me ^ distance))
-                        def _():
-                            pltpu.make_async_copy(
-                                cl.at[pl.ds(index, 1), :], cloud_hbm[distance].at[pl.ds(rank, 1), :], sem_cloud.at[index]
-                            ).start()
-
-            return inner
-
-        lax.fori_loop(0, ROWS, store, 0)
+                    pltpu.make_async_copy(
+                        cl.at[pl.ds(index, 1), :], cloud_hbm[distance].at[pl.ds(rank, 1), :], sem_cloud.at[index]
+                    ).start()
+
+        for member in range(ROWS):
+            if member < (slots - 1) % ROWS + 1:
+                store(member)
+            else:
+                pl.when(group < groups - 1)(functools.partial(store, member))
         return carry
 
     lax.fori_loop(0, groups, run_group, 0)
 
-    def finish(index, carry):
+    for index in range(slots):
         pltpu.make_async_copy(xs.at[:, pl.ds(index, 1), :], y_hbm.at[:, pl.ds(0, 1), :], sem_out.at[index]).wait()
-
-        @pl.when(meta_s[1, index] > 0)
-        def _():
-            pltpu.make_async_copy(cl.at[pl.ds(index, 1), :], cloud_hbm[0].at[pl.ds(0, 1), :], sem_cloud.at[index]).wait()
-
-        return carry
-
-    lax.fori_loop(0, slots, finish, 0)
+        pltpu.make_async_copy(cl.at[pl.ds(index, 1), :], cloud_hbm[0].at[pl.ds(0, 1), :], sem_cloud.at[index]).wait()
 
 
 def run_models(row_blocks, state, levels):
@@ -394,7 +381,7 @@
             pltpu.VMEM((ROWS, LANES), jnp.int32),
             pltpu.SMEM((ROWS, LANES), jnp.int32),
             pltpu.SemaphoreType.DMA,
-            pltpu.SemaphoreType.DMA((slots,)),
+            pltpu.SemaphoreType.DMA((groups,)),
             pltpu.SemaphoreType.DMA((slots,)),
             pltpu.SemaphoreType.DMA((slots,)),
         ],
@@ -504,12 +491,14 @@
     row_blocks = exchange([rows] * workers, "crm")
     state, tendency, clouds = run_models(row_blocks, crm_state.transpose(1, 0, 2), levels)
     tendencies = exchange([tendency] * workers, "crm")
+    clouds, tendencies = lax.optimization_barrier((clouds, tendencies))
 
     edge = pl.pallas_call(
         functools.partial(edge_kernel, levels, columns, workers),
         out_shape=jax.ShapeDtypeStruct((columns, LANES), F32),
         in_specs=[vmem] * workers,
         out_specs=vmem,
+        compiler_params=pltpu.CompilerParams(vmem_limit_bytes=8 * MIB),
         name="edge_columns",
     )(*tendencies)
     pairs = []
@@ -525,6 +514,7 @@
         in_specs=[pl.BlockSpec(memory_space=pltpu.SMEM)] + [hbm] * workers,
         out_specs=hbm,
         scratch_shapes=[pltpu.SMEM((workers,), jnp.int32), pltpu.SemaphoreType.DMA((columns,))],
+        compiler_params=pltpu.CompilerParams(vmem_limit_bytes=8 * MIB),
         name="cloud_rows",
     )(target, *clouds)
     physics = pl.pallas_call(
@@ -532,6 +522,7 @@
         out_shape=jax.ShapeDtypeStruct((columns, 2, gcm), F32),
         in_specs=[vmem] * (workers + 4),
         out_specs=vmem,
+        compiler_params=pltpu.CompilerParams(vmem_limit_bytes=8 * MIB),
         name="physics_cells",
     )(*tendencies, edge, remap_index.T, remap_weight.T, level_map)
     return state.transpose(1, 0, 2), cloud_water, physics

time: 69.8 us -> 46.5 us (0.67)
  Pallas kernels: 30.9 us -> 16.2 us
  waiting for transfers between devices: 17.1 us -> 9.95 us
  local copies, waits for them, and re-layouts: 5.46 us -> 4.29 us
    pallas_call x1, Pallas kernels: 12.8 us -> 1.77 us  [body(): pl.pallas_call(functools.partial(cloud_kernel, columns, workers), out_sha...]
    ppermute x9, waiting for transfers between devices: 12.5 us -> 5 us  [exchange(): lax.ppermute(blocks[distance], axis, [(i, i ^ distance) for i in range(si...]
    pallas_call x1, Pallas kernels: 1.78 us -> 0.4 us  [body(): pl.pallas_call(functools.partial(edge_kernel, levels, columns, workers),...]
    unnamed x22 -> x18, local copies, waits for them, and re-layouts: 5.46 us -> 4.29 us
    ppermute x9, starting transfers between devices: 11 us -> 10.1 us  [exchange(): lax.ppermute(blocks[distance], axis, [(i, i ^ distance) for i in range(si...]
    pallas_call x1, Pallas kernels: 2.34 us -> 1.47 us  [body(): pl.pallas_call(functools.partial(physics_kernel, levels, columns, workers...]
    pallas_call x1, Pallas kernels: 1.99 us -> 1.14 us  [pack(): pl.pallas_call(functools.partial(pack_kernel, capacity, workers), out_sha...]
    ppermute x1, starting transfers between devices: 3.82 us -> 4.57 us  [body(): edge = lax.ppermute(edge, ('grp', 'crm'), pairs)]
  transfers between devices with their start and end apart: 10 -> 10, of which waited for: 5 -> 4; matrix products, arithmetic and copies ran while one was open for 0% -> 0% of each run, Pallas kernels for 6% -> 4%
where the time goes in v2:
time: 46.5 us; the launch traced here: 45.8 us
  Pallas kernels  16.2 us (35%)
  starting transfers between devices  14.7 us (32%)
  waiting for transfers between devices  9.95 us (21%)
  local copies, waits for them, and re-layouts  4.29 us (9%)
  between operations  0.71 us (2%)
    pallas_call x1, Pallas kernels, run_models(): pl.pallas_call(functools.partial(model_kernel, workers, slots, levels, wi...  11.4 us
    ppermute x9, starting transfers between devices, exchange(): lax.ppermute(blocks[distance], axis, [(i, i ^ distance) for i in range(si...  10.1 us
    ppermute x9, waiting for transfers between devices, exchange(): lax.ppermute(blocks[distance], axis, [(i, i ^ distance) for i in range(si...  5 us
    ppermute x1, waiting for transfers between devices, body(): edge = lax.ppermute(edge, ('grp', 'crm'), pairs)  4.95 us
    ppermute x1, starting transfers between devices, body(): edge = lax.ppermute(edge, ('grp', 'crm'), pairs)  4.57 us
    unnamed x18, local copies, waits for them, and re-layouts  4.29 us
    pallas_call x1, Pallas kernels, body(): pl.pallas_call(functools.partial(cloud_kernel, columns, workers), out_sha...  1.77 us
    pallas_call x1, Pallas kernels, body(): pl.pallas_call(functools.partial(physics_kernel, levels, columns, workers...  1.47 us
  transfers between devices with their start and end apart: 10, of which 4 were waited for; matrix products, arithmetic and copies ran while one was open for 0% of the time, Pallas kernels for 4%

profile of v2, /device:TPU:0, one launch (start us, length us, event | category | flops | bytes accessed | tf_op | source)
XLA Modules:
  0.0 45.8 jit_solution(13746986202894654903)
XLA Ops:
  0.6 0.0 copy-start.1
  0.6 0.7 %copy-done.1 = f32[58,72]{1,0:T(8,128)S(1)} copy-done((f32[58,72]{1,0:T(8,128)S(1)}, f32[58,72]{1,0:T(8,128)}, u32[]{:S(2)}) %copy-start.1) | copy-done | bytes 16728
  1.4 0.0 copy-start.3
  1.4 0.7 %copy-done.3 = f32[24,2,72]{2,1,0:T(2,128)S(1)} copy-done((f32[24,2,72]{2,1,0:T(2,128)S(1)}, f32[24,2,72]{2,1,0:T(2,128)}, u32[]{:S(2)}) %copy-start.3) | copy-done | bytes 13848
  2.1 0.0 copy-start.6
  2.1 0.7 %copy-done.6 = s32[24]{0:T(128)S(1)} copy-done((s32[24]{0:T(128)S(1)}, s32[24]{0:T(128)}, u32[]{:S(2)}) %copy-start.6) | copy-done | bytes 120
  2.8 0.0 copy-start.8
  2.8 0.7 %copy-done.8 = s32[24]{0:T(128)S(1)} copy-done((s32[24]{0:T(128)S(1)}, s32[24]{0:T(128)}, u32[]{:S(2)}) %copy-start.8) | copy-done | bytes 120
  3.4 0.0 copy-start.2
  3.4 0.0 copy-start.4
  3.4 0.0 copy-start.5
  3.4 0.0 copy-start.7
  3.5 1.1 %pack_forcing.1.refs_0_ = f32[24,128]{1,0:T(8,128)S(1)} custom-call(s32[24]{0:T(128)S(1)} %copy-done.6, s32[24]{0:T(128)S(1)} %copy-done.8, f32[24,2,72]{2,1,0:T(2,128)S(1)} %copy-done.3, f32[58,72]{1,0:T(8,128)S(1)} %copy-done.1), custom_call_target="tpu_custom_call" | custom-call | tf_op jit(solution)/shard_map/pack_forcing/pallas_call | solution.py:81
  4.6 2.4 %collective-permute-start.2 = (f32[24,128]{1,0:T(8,128)S(1)}, f32[24,128]{1,0:T(8,128)S(1)}, u32[]{:S(2)}, u32[]{:S(2)}) collective-permute-start(f32[24,128]{1,0:T(8,128)S(1)} %pack_forcing.1.refs_0_), channel_id=1, source_target_pairs={{0,3},{1,2},{2,1},{3,0},{4,7},{5,6},{6,5},{7,4},{8,11},{9,10},{10,... | collective-permute-start | bytes 36872 | tf_op jit(solution)/shard_map/ppermute | solution.py:476
  7.0 0.6 %collective-permute-start.1 = (f32[24,128]{1,0:T(8,128)S(1)}, f32[24,128]{1,0:T(8,128)S(1)}, u32[]{:S(2)}, u32[]{:S(2)}) collective-permute-start(f32[24,128]{1,0:T(8,128)S(1)} %pack_forcing.1.refs_0_), channel_id=1, source_target_pairs={{0,2},{1,3},{2,0},{3,1},{4,6},{5,7},{6,4},{7,5},{8,10},{9,11},{10,... | collective-permute-start | bytes 36872 | tf_op jit(solution)/shard_map/ppermute | solution.py:476
  7.7 0.0 collective-permute-start
  7.7 0.7 %collective-permute-done.2.refs_3_ = f32[24,128]{1,0:T(8,128)S(1)} collective-permute-done((f32[24,128]{1,0:T(8,128)S(1)}, f32[24,128]{1,0:T(8,128)S(1)}, u32[]{:S(2)}, u32[]{:S(2)}) %collective-permute-start.2) | collective-permute-done | bytes 12320 | tf_op jit(solution)/shard_map/ppermute | solution.py:476
  8.4 2.3 %collective-permute-done.1.refs_2_ = f32[24,128]{1,0:T(8,128)S(1)} collective-permute-done((f32[24,128]{1,0:T(8,128)S(1)}, f32[24,128]{1,0:T(8,128)S(1)}, u32[]{:S(2)}, u32[]{:S(2)}) %collective-permute-start.1) | collective-permute-done | bytes 12320 | tf_op jit(solution)/shard_map/ppermute | solution.py:476
  10.7 0.0 collective-permute-done.refs_1_
  10.7 0.0 copy-start
  10.7 1.5 %copy-done = f32[36,3,3712]{2,0,1:T(8,128)S(1)} copy-done((f32[36,3,3712]{2,0,1:T(8,128)S(1)}, f32[36,3,3712]{2,0,1:T(8,128)}, u32[]{:S(2)}) %copy-start) | copy-done | bytes 1603608
  12.2 11.4 %cloud_models.1 = (f32[3,36,3712]{2,1,0:T(8,128)}, f32[40,128]{1,0:T(8,128)S(1)}, f32[9,3712]{1,0:T(8,128)S(1)}, f32[9,3712]{1,0:T(8,128)S(1)}, f32[9,3712]{1,0:T(8,128)S(1)}, /*index=5*/f32[9,3712]{1,0:T(8,128)S(1)}) custom-call(f32[24,128]{1,0:T(8,128)S(1)} %pack_forcing.1.refs_0_, f32[24,128]{1,0:T(8,128)S(1)} %collective-permute-done.refs_1_, ...), custom_call_target="tpu_custom_call" | custom-call | tf_op jit(solution)/shard_map/cloud_models/pallas_call | solution.py:366
  23.6 0.1 collective-permute-start.5
  23.7 5.0 %collective-permute-start.4 = (f32[40,128]{1,0:T(8,128)S(1)}, f32[40,128]{1,0:T(8,128)S(1)}, u32[]{:S(2)}, u32[]{:S(2)}) collective-permute-start(f32[40,128]{1,0:T(8,128)S(1)} %get-tuple-element.27.refs_0_), channel_id=1, source_target_pairs={{0,2},{1,3},{2,0},{3,1},{4,6},{5,7},{6,4},{7,5},{8,10},{9,11},{10,... | collective-permute-start | bytes 61448 | tf_op jit(solution)/shard_map/ppermute | solution.py:476
  28.7 0.0 collective-permute-start.3
  28.7 0.0 collective-permute-done.5.refs_3_
  28.7 2.0 %collective-permute-done.4.refs_2_ = f32[40,128]{1,0:T(8,128)S(1)} collective-permute-done((f32[40,128]{1,0:T(8,128)S(1)}, f32[40,128]{1,0:T(8,128)S(1)}, u32[]{:S(2)}, u32[]{:S(2)}) %collective-permute-start.4) | collective-permute-done | bytes 20512 | tf_op jit(solution)/shard_map/ppermute | solution.py:476
  30.7 0.0 collective-permute-done.3.refs_1_
  30.7 0.0 collective-permute-start.6
  30.7 1.8 %collective-permute-start.7 = (f32[9,3712]{1,0:T(8,128)S(1)}, f32[9,3712]{1,0:T(8,128)S(1)}, u32[]{:S(2)}, u32[]{:S(2)}) collective-permute-start(f32[9,3712]{1,0:T(8,128)S(1)} %get-tuple-element.25), channel_id=1, source_target_pairs={{0,2},{1,3},{2,0},{3,1},{4,6},{5,7},{6,4},{7,5},{8,10},{9,11},{10,... | collective-permute-start | bytes 400904 | tf_op jit(solution)/shard_map/ppermute | solution.py:476
  32.5 0.1 collective-permute-start.8
  32.6 0.4 edge_columns.1
  33.0 4.6 %collective-permute-start.9 = (f32[24,128]{1,0:T(8,128)S(1)}, f32[24,128]{1,0:T(8,128)S(1)}, u32[]{:S(2)}, u32[]{:S(2)}) collective-permute-start(f32[24,128]{1,0:T(8,128)S(1)} %edge_columns.1), channel_id=1, source_target_pairs={{0,4},{7,3},{4,8},{11,7},{8,12},{15,11},{12,16},{19,15},{16,20},{2... | collective-permute-start | bytes 36872 | tf_op jit(solution)/shard_map/ppermute | solution.py:509
  37.6 5.0 %collective-permute-done.9.refs_4_ = f32[24,128]{1,0:T(8,128)S(1)} collective-permute-done((f32[24,128]{1,0:T(8,128)S(1)}, f32[24,128]{1,0:T(8,128)S(1)}, u32[]{:S(2)}, u32[]{:S(2)}) %collective-permute-start.9) | collective-permute-done | bytes 12320 | tf_op jit(solution)/shard_map/ppermute | solution.py:509
  42.6 0.0 copy-done.2
  42.6 0.0 copy-done.4
  42.6 0.0 copy-done.5
  42.6 1.5 %physics_cells.1 = f32[24,2,72]{2,1,0:T(2,128)} custom-call(f32[40,128]{1,0:T(8,128)S(1)} %get-tuple-element.27.refs_0_, f32[40,128]{1,0:T(8,128)S(1)} %collective-permute-done.3.refs_1_, f32[40,128]{1,0:T(8,128)S(1)} %collective-permute-done.4.refs_2_, f32[40,128]{1,0:T(8,128)S(1)} %collective-permute-done.5.refs_3_, ...), custom_call_target="tpu_custom_call" | custom-call | tf_op jit(solution)/shard_map/physics_cells/pallas_call | solution.py:520
  44.0 0.0 collective-permute-done.6.refs_2_
  44.0 0.0 collective-permute-done.7.refs_3_
  44.0 0.0 collective-permute-done.8.refs_4_
  44.0 0.0 copy-done.7
  44.1 1.8 %cloud_rows.1 = f32[24,3712]{1,0:T(8,128)} custom-call(s32[24]{0:T(128)S(1)} %copy-done.7, f32[9,3712]{1,0:T(8,128)S(1)} %get-tuple-element.23.refs_1_, f32[9,3712]{1,0:T(8,128)S(1)} %collective-permute-done.6.refs_2_, f32[9,3712]{1,0:T(8,128)S(1)} %collective-permute-done.7.refs_3_, f32[9,3712]{1,0:T(8,128)S(1)} %collective-permute-done.8.refs_4_), custom_call_target="tpu_custom_call" | custom-call | tf_op jit(solution)/shard_map/cloud_rows/pallas_call | solution.py:511
Async XLA Ops:
  0.6 0.8 %copy-start.1 = (f32[58,72]{1,0:T(8,128)S(1)}, f32[58,72]{1,0:T(8,128)}, u32[]{:S(2)}) copy-start(f32[58,72]{1,0:T(8,128)} %refs_7_.1) | copy-start | bytes 50116
  1.4 0.7 %copy-start.3 = (f32[24,2,72]{2,1,0:T(2,128)S(1)}, f32[24,2,72]{2,1,0:T(2,128)}, u32[]{:S(2)}) copy-start(f32[24,2,72]{2,1,0:T(2,128)} %forcing.1) | copy-start | bytes 41476
  2.1 0.7 %copy-start.6 = (s32[24]{0:T(128)S(1)}, s32[24]{0:T(128)}, u32[]{:S(2)}) copy-start(s32[24]{0:T(128)} %refs_0_.1) | copy-start | bytes 292
  2.8 0.7 %copy-start.8 = (s32[24]{0:T(128)S(1)}, s32[24]{0:T(128)}, u32[]{:S(2)}) copy-start(s32[24]{0:T(128)} %cost.1) | copy-start | bytes 292
  3.4 39.1 %copy-start.2 = (f32[58,72]{1,0:T(8,128)S(1)}, f32[58,72]{1,0:T(8,128)}, u32[]{:S(2)}) copy-start(f32[58,72]{1,0:T(8,128)} %refs_7_.1) | copy-start | bytes 50116
  3.4 39.1 %copy-start.4 = (s32[24,4]{0,1:T(4,128)S(1)}, s32[24,4]{0,1:T(4,128)}, u32[]{:S(2)}) copy-start(s32[24,4]{0,1:T(4,128)} %param.12) | copy-start | bytes 1156
  3.4 39.1 %copy-start.5 = (f32[24,4]{0,1:T(4,128)S(1)}, f32[24,4]{0,1:T(4,128)}, u32[]{:S(2)}) copy-start(f32[24,4]{0,1:T(4,128)} %param.13) | copy-start | bytes 1156
  3.4 40.6 %copy-start.7 = (s32[24]{0:T(128)S(1)}, s32[24]{0:T(128)}, u32[]{:S(2)}) copy-start(s32[24]{0:T(128)} %refs_0_.1) | copy-start | bytes 292
  4.6 3.8 %collective-permute-start.2 = (f32[24,128]{1,0:T(8,128)S(1)}, f32[24,128]{1,0:T(8,128)S(1)}, u32[]{:S(2)}, u32[]{:S(2)}) collective-permute-start(f32[24,128]{1,0:T(8,128)S(1)} %pack_forcing.1.refs_0_), channel_id=1, source_target_pairs={{0,3},{1,2},{2,1},{3,0},{4,7},{5,6},{6,5},{7,4},{8,11},{9,10},{10,... | collective-permute-start | bytes 36872 | tf_op jit(solution)/shard_map/ppermute | solution.py:476
  7.0 3.7 %collective-permute-start.1 = (f32[24,128]{1,0:T(8,128)S(1)}, f32[24,128]{1,0:T(8,128)S(1)}, u32[]{:S(2)}, u32[]{:S(2)}) collective-permute-start(f32[24,128]{1,0:T(8,128)S(1)} %pack_forcing.1.refs_0_), channel_id=1, source_target_pairs={{0,2},{1,3},{2,0},{3,1},{4,6},{5,7},{6,4},{7,5},{8,10},{9,11},{10,... | collective-permute-start | bytes 36872 | tf_op jit(solution)/shard_map/ppermute | solution.py:476
  7.7 3.1 %collective-permute-start = (f32[24,128]{1,0:T(8,128)S(1)}, f32[24,128]{1,0:T(8,128)S(1)}, u32[]{:S(2)}, u32[]{:S(2)}) collective-permute-start(f32[24,128]{1,0:T(8,128)S(1)} %pack_forcing.1.refs_0_), channel_id=1, source_target_pairs={{0,1},{1,0},{2,3},{3,2},{4,5},{5,4},{6,7},{7,6},{8,9},{9,8},{10,11... | collective-permute-start | bytes 36872 | tf_op jit(solution)/shard_map/ppermute | solution.py:476
  10.7 1.5 %copy-start = (f32[36,3,3712]{2,0,1:T(8,128)S(1)}, f32[36,3,3712]{2,0,1:T(8,128)}, u32[]{:S(2)}) copy-start(f32[36,3,3712]{2,0,1:T(8,128)} %param.7) | copy-start | bytes 4810756
  23.6 5.1 %collective-permute-start.5 = (f32[40,128]{1,0:T(8,128)S(1)}, f32[40,128]{1,0:T(8,128)S(1)}, u32[]{:S(2)}, u32[]{:S(2)}) collective-permute-start(f32[40,128]{1,0:T(8,128)S(1)} %get-tuple-element.27.refs_0_), channel_id=1, source_target_pairs={{0,3},{1,2},{2,1},{3,0},{4,7},{5,6},{6,5},{7,4},{8,11},{9,10},{10,... | collective-permute-start | bytes 61448 | tf_op jit(solution)/shard_map/ppermute | solution.py:476
  23.7 7.0 %collective-permute-start.4 = (f32[40,128]{1,0:T(8,128)S(1)}, f32[40,128]{1,0:T(8,128)S(1)}, u32[]{:S(2)}, u32[]{:S(2)}) collective-permute-start(f32[40,128]{1,0:T(8,128)S(1)} %get-tuple-element.27.refs_0_), channel_id=1, source_target_pairs={{0,2},{1,3},{2,0},{3,1},{4,6},{5,7},{6,4},{7,5},{8,10},{9,11},{10,... | collective-permute-start | bytes 61448 | tf_op jit(solution)/shard_map/ppermute | solution.py:476
  28.7 2.0 %collective-permute-start.3 = (f32[40,128]{1,0:T(8,128)S(1)}, f32[40,128]{1,0:T(8,128)S(1)}, u32[]{:S(2)}, u32[]{:S(2)}) collective-permute-start(f32[40,128]{1,0:T(8,128)S(1)} %get-tuple-element.27.refs_0_), channel_id=1, source_target_pairs={{0,1},{1,0},{2,3},{3,2},{4,5},{5,4},{6,7},{7,6},{8,9},{9,8},{10,11... | collective-permute-start | bytes 61448 | tf_op jit(solution)/shard_map/ppermute | solution.py:476
  30.7 13.4 %collective-permute-start.6 = (f32[9,3712]{1,0:T(8,128)S(1)}, f32[9,3712]{1,0:T(8,128)S(1)}, u32[]{:S(2)}, u32[]{:S(2)}) collective-permute-start(f32[9,3712]{1,0:T(8,128)S(1)} %get-tuple-element.24), channel_id=1, source_target_pairs={{0,1},{1,0},{2,3},{3,2},{4,5},{5,4},{6,7},{7,6},{8,9},{9,8},{10,11... | collective-permute-start | bytes 400904 | tf_op jit(solution)/shard_map/ppermute | solution.py:476
  30.7 13.4 %collective-permute-start.7 = (f32[9,3712]{1,0:T(8,128)S(1)}, f32[9,3712]{1,0:T(8,128)S(1)}, u32[]{:S(2)}, u32[]{:S(2)}) collective-permute-start(f32[9,3712]{1,0:T(8,128)S(1)} %get-tuple-element.25), channel_id=1, source_target_pairs={{0,2},{1,3},{2,0},{3,1},{4,6},{5,7},{6,4},{7,5},{8,10},{9,11},{10,... | collective-permute-start | bytes 400904 | tf_op jit(solution)/shard_map/ppermute | solution.py:476
  32.5 11.6 %collective-permute-start.8 = (f32[9,3712]{1,0:T(8,128)S(1)}, f32[9,3712]{1,0:T(8,128)S(1)}, u32[]{:S(2)}, u32[]{:S(2)}) collective-permute-start(f32[9,3712]{1,0:T(8,128)S(1)} %get-tuple-element.26), channel_id=1, source_target_pairs={{0,3},{1,2},{2,1},{3,0},{4,7},{5,6},{6,5},{7,4},{8,11},{9,10},{10,... | collective-permute-start | bytes 400904 | tf_op jit(solution)/shard_map/ppermute | solution.py:476
  33.0 9.5 %collective-permute-start.9 = (f32[24,128]{1,0:T(8,128)S(1)}, f32[24,128]{1,0:T(8,128)S(1)}, u32[]{:S(2)}, u32[]{:S(2)}) collective-permute-start(f32[24,128]{1,0:T(8,128)S(1)} %edge_columns.1), channel_id=1, source_target_pairs={{0,4},{7,3},{4,8},{11,7},{8,12},{15,11},{12,16},{19,15},{16,20},{2... | collective-permute-start | bytes 36872 | tf_op jit(solution)/shard_map/ppermute | solution.py:509
